TPU v7x, 32 devices: a whole 2x2x4 slice. The times are simulated.
32 devices in a mesh: dp: 8 (over y, x, core), mp: 4 (over z).
Axes of the slice: x: 2, y: 2, z: 4, core: 2. Of those that a mesh axis runs over, the one named last changes fastest.
Arguments:
- inputs: float32 [8192, 768], P(('dp', 'mp')), may hold values from -6 to 6
- cotangent: float32 [8192, 768], P(('dp', 'mp')), may hold values from -0.5 to 0.5
- loss_mask: int32 [8192], P(('dp', 'mp')), may hold values from 0 to 1, as said below
- keep_mask: int32 [8], P('dp'), may hold values 0 or 1
- w_qkv: float32 [2, 3, 768, 768], P(None, None, None, 'mp'), may hold values from -0.21875 to 0.21875
- w_out: float32 [2, 768, 768], P(None, 'mp'), may hold values from -1.75 to 1.75
- w_in: float32 [2, 768, 3072], P(None, None, 'mp'), may hold values from -0.21875 to 0.21875
- w_down: float32 [2, 3072, 768], P(None, 'mp'), may hold values from -0.109375 to 0.109375
- norm_params: float32 [2, 2, 2, 768], replicated, may hold values from -1 to 1.5, as said below
- norm_moments: float32 [2, 2, 2, 768], replicated, may hold values from 0.11 to 0.45
- left_stats: float32 [1536, 96, 96], P(('dp', 'mp')), may hold values from -8 to 43, as said below
- right_stats: float32 [1536, 96, 96], P(('dp', 'mp')), may hold values from -8 to 43, as said below
- left_roots: float32 [1536, 96, 96], P(('dp', 'mp')), may hold values from -1 to 2, as said below
- right_roots: float32 [1536, 96, 96], P(('dp', 'mp')), may hold values from -1 to 2, as said below
Outputs:
- outputs: float32 [8192, 768], P(('dp', 'mp'))
- in_grads: float32 [8192, 768], P(('dp', 'mp'))
- block_grads: float32 [1536, 96, 96], P(('dp', 'mp'))
- left_new: float32 [1536, 96, 96], P(('dp', 'mp'))
- right_new: float32 [1536, 96, 96], P(('dp', 'mp'))
- qkv_new: float32 [2, 3, 768, 768], P(None, None, None, 'mp')
- out_new: float32 [2, 768, 768], P(None, 'mp')
- in_new: float32 [2, 768, 3072], P(None, None, 'mp')
- down_new: float32 [2, 3072, 768], P(None, 'mp')
- norm_grads: float32 [2, 2, 2, 768], replicated
- moments_new: float32 [2, 2, 2, 768], replicated
- norms_new: float32 [2, 2, 2, 768], replicated
Inputs may be any that keep to these rules, and one draw needn't show every extreme that they name: `loss_mask`: each sequence's tokens are 1 with a chance of 5 to 25 percent drawn for that sequence. `norm_params`: gains near 1, biases near 0. `left_stats`: each block is symmetric. `right_stats`: each block is symmetric. `left_roots`: each block is symmetric. `right_roots`: each block is symmetric.
All inputs are finite; a program needn't handle non-finite values. No bound on the sum of `keep_mask` on one device may be relied on, other than what follows from the above.
Results may differ from a plain program's by a relative error of at most 0.0003.
Values sent between devices are 32-bit elements; how exact they have to be, the bound alone decides.
A program may use at most 256 MiB of HBM per device.

v0:
```python
import math

import jax
import jax.numpy as jnp
from jax import lax
from jax.sharding import PartitionSpec as P

HEAD = 64
LEN = 1024
BLOCK = 96


HIGHEST = lax.Precision.HIGHEST
norm_eps = 1e-05
stat_decay = 0.9
shampoo_rate = 0.02
graft_eps = 1e-06
moment_decay = 0.9
vector_rate = 0.05
vector_eps = 1e-08
sqrt_half = 0.7071067811865476
inv_sqrt_tau = 0.3989422804014327


def matmul(left_op, right_op):
    return jnp.dot(left_op, right_op, precision=HIGHEST)


def matmul_t(left_op, right_op):
    return jnp.einsum("sa,ba->sb", left_op, right_op, precision=HIGHEST)


def inner_rows(left_op, right_op):
    return jnp.einsum("sa,sb->ab", left_op, right_op, precision=HIGHEST)


def gather_rows(local_rows):
    return lax.all_gather(local_rows, "mp", axis=0, tiled=True)


def reduce_rows(partial_value):
    return lax.psum_scatter(partial_value, "mp", scatter_dimension=0, tiled=True)


def gather_grads(local_rows):
    return lax.all_gather(local_rows, "mp", axis=0, tiled=True)


def reduce_grads(partial_value):
    return lax.psum_scatter(partial_value, "mp", scatter_dimension=0, tiled=True)


def norm_forward(hidden, gain_vec, bias_vec):
    center = jnp.mean(hidden, axis=-1, keepdims=True)
    shifted = hidden - center
    spread = jnp.mean(shifted * shifted, axis=-1, keepdims=True)
    inv_scale = lax.rsqrt(spread + norm_eps)
    normed = shifted * inv_scale
    return (normed * gain_vec + bias_vec, normed, inv_scale)


def norm_backward(upstream, normed, inv_scale, gain_vec):
    scaled = upstream * gain_vec
    return inv_scale * (
        scaled
        - jnp.mean(scaled, axis=-1, keepdims=True)
        - normed * jnp.mean(scaled * normed, axis=-1, keepdims=True)
    )


def gelu_value(pre_act):
    return 0.5 * pre_act * (1.0 + lax.erf(pre_act * sqrt_half))


def gelu_slope(pre_act):
    return (
        0.5 * (1.0 + lax.erf(pre_act * sqrt_half))
        + pre_act * jnp.exp(-0.5 * pre_act * pre_act) * inv_sqrt_tau
    )


def attend_forward(queries, key_rows, value_rows):
    score_scale = queries.shape[-1] ** (-0.5)

    def single_seq(seq_item):
        query_seq, key_seq, value_seq = seq_item
        scores = jnp.einsum("qhd,khd->hqk", query_seq, key_seq, precision=HIGHEST) * score_scale
        row_peak = jnp.max(scores, axis=-1, keepdims=True)
        exp_scores = jnp.exp(scores - row_peak)
        totals = jnp.sum(exp_scores, axis=-1, keepdims=True)
        context = jnp.einsum("hqk,khd->qhd", exp_scores / totals, value_seq, precision=HIGHEST)
        return (context, (row_peak + jnp.log(totals))[..., 0])

    return lax.map(single_seq, (queries, key_rows, value_rows))


def attend_backward(queries, key_rows, value_rows, context, log_totals, grad_context):
    score_scale = queries.shape[-1] ** (-0.5)

    def single_seq(seq_item):
        query_seq, key_seq, value_seq, context_seq, lse_seq, grad_seq = seq_item
        scores = jnp.einsum("qhd,khd->hqk", query_seq, key_seq, precision=HIGHEST) * score_scale
        attn_probs = jnp.exp(scores - lse_seq[..., None])
        grad_value = jnp.einsum("hqk,qhd->khd", attn_probs, grad_seq, precision=HIGHEST)
        grad_probs = jnp.einsum("qhd,khd->hqk", grad_seq, value_seq, precision=HIGHEST)
        row_dot = jnp.swapaxes(jnp.sum(grad_seq * context_seq, axis=-1), 0, 1)
        grad_scores = attn_probs * (grad_probs - row_dot[..., None]) * score_scale
        grad_query = jnp.einsum("hqk,khd->qhd", grad_scores, key_seq, precision=HIGHEST)
        grad_key = jnp.einsum("hqk,qhd->khd", grad_scores, query_seq, precision=HIGHEST)
        return (grad_query, grad_key, grad_value)

    return lax.map(single_seq, (queries, key_rows, value_rows, context, log_totals, grad_context))


def layer_forward(local_in, qkv_layer, out_layer, in_layer, down_layer, norm_set):
    full_in = gather_rows(local_in)
    rows_all = full_in.shape[0]
    width_loc = qkv_layer.shape[2]
    projected = jnp.einsum("sd,cde->cse", full_in, qkv_layer, precision=HIGHEST)
    shaped = projected.reshape(3, rows_all // LEN, LEN, width_loc // HEAD, HEAD)
    context, log_totals = attend_forward(shaped[0], shaped[1], shaped[2])
    context_rows = context.reshape(rows_all, width_loc)
    attn_part = reduce_rows(matmul(context_rows, out_layer))
    middle, normed_one, scale_one = norm_forward(
        local_in + attn_part, norm_set[0, 0], norm_set[0, 1]
    )
    full_mid = gather_rows(middle)
    pre_act = matmul(full_mid, in_layer)
    activated = gelu_value(pre_act)
    ffn_part = reduce_rows(matmul(activated, down_layer))
    result, normed_two, scale_two = norm_forward(middle + ffn_part, norm_set[1, 0], norm_set[1, 1])
    kept_set = (
        full_in,
        shaped,
        context_rows,
        log_totals,
        normed_one,
        scale_one,
        full_mid,
        pre_act,
        activated,
        normed_two,
        scale_two,
        local_in,
        middle,
    )
    return (result, kept_set)


def layer_backward(grad_top, kept_set, qkv_layer, out_layer, in_layer, down_layer, norm_set):
    (
        full_in,
        shaped,
        context_rows,
        log_totals,
        normed_one,
        scale_one,
        full_mid,
        pre_act,
        activated,
        normed_two,
        scale_two,
        local_in,
        middle,
    ) = kept_set
    rows_all = context_rows.shape[0]
    width_loc = context_rows.shape[1]
    grad_gain_two = jnp.sum(grad_top * normed_two, axis=0)
    grad_bias_two = jnp.sum(grad_top, axis=0)
    grad_second = norm_backward(grad_top, normed_two, scale_two, norm_set[1, 0])
    grad_full = gather_grads(grad_second)
    grad_act = matmul_t(grad_full, down_layer)
    grad_down = inner_rows(activated, grad_full)
    grad_pre = grad_act * gelu_slope(pre_act)
    grad_in = inner_rows(full_mid, grad_pre)
    grad_middle = grad_second + reduce_grads(matmul_t(grad_pre, in_layer))
    grad_gain_one = jnp.sum(grad_middle * normed_one, axis=0)
    grad_bias_one = jnp.sum(grad_middle, axis=0)
    grad_attn_local = norm_backward(grad_middle, normed_one, scale_one, norm_set[0, 0])
    grad_attn = gather_grads(grad_attn_local)
    grad_context = matmul_t(grad_attn, out_layer)
    grad_outw = inner_rows(context_rows, grad_attn)
    context = context_rows.reshape(shaped[0].shape)
    grad_query, grad_key, grad_value = attend_backward(
        shaped[0], shaped[1], shaped[2], context, log_totals, grad_context.reshape(shaped[0].shape)
    )
    grad_proj = jnp.stack(
        [
            grad_query.reshape(rows_all, width_loc),
            grad_key.reshape(rows_all, width_loc),
            grad_value.reshape(rows_all, width_loc),
        ]
    )
    grad_qkv = jnp.einsum("sd,cse->cde", full_in, grad_proj, precision=HIGHEST)
    grad_local = grad_attn_local + reduce_grads(
        jnp.einsum("cse,cde->sd", grad_proj, qkv_layer, precision=HIGHEST)
    )
    norm_grads = jnp.stack(
        [jnp.stack([grad_gain_one, grad_bias_one]), jnp.stack([grad_gain_two, grad_bias_two])]
    )
    return (grad_local, (grad_qkv, grad_outw, grad_in, grad_down), norm_grads)


def cut_blocks(matrix):
    leading = tuple(matrix.shape[:-2])
    row_count, col_count = matrix.shape[-2:]
    tiled = matrix.reshape(leading + (row_count // BLOCK, BLOCK, col_count // BLOCK, BLOCK))
    return jnp.swapaxes(tiled, -3, -2).reshape(-1, BLOCK, BLOCK)


def tile_blocks(qkv_part, out_part, in_part, down_part):
    return jnp.concatenate(
        [cut_blocks(qkv_part), cut_blocks(out_part), cut_blocks(in_part), cut_blocks(down_part)],
        axis=0,
    )


def join_blocks(blocks, target_shape):
    leading = tuple(target_shape[:-2])
    row_count, col_count = target_shape[-2:]
    tiled = blocks.reshape(leading + (row_count // BLOCK, col_count // BLOCK, BLOCK, BLOCK))
    return jnp.swapaxes(tiled, -3, -2).reshape(target_shape)


def untile_blocks(blocks, shape_list):
    pieces = []
    offset = 0
    for target_shape in shape_list:
        block_count = math.prod(target_shape) // (BLOCK * BLOCK)
        pieces.append(join_blocks(blocks[offset : offset + block_count], target_shape))
        offset = offset + block_count
    return pieces


def on_device(
    inputs,
    cotangent,
    loss_mask,
    keep_mask,
    w_qkv,
    w_out,
    w_in,
    w_down,
    norm_params,
    norm_moments,
    left_stats,
    right_stats,
    left_roots,
    right_roots,
):
    rows_loc = inputs.shape[0]
    seqs_loc = keep_mask.shape[0]
    row_index = lax.axis_index("mp") * rows_loc + jnp.arange(rows_loc, dtype=jnp.int32)
    seq_ids = row_index // LEN
    matches = seq_ids[:, None] == jnp.arange(seqs_loc, dtype=jnp.int32)[None, :]
    keep_rows = jnp.sum(jnp.where(matches, keep_mask[None, :], 0), axis=1).astype(jnp.float32)[
        :, None
    ]
    first_out, kept_one = layer_forward(
        inputs, w_qkv[0], w_out[0], w_in[0], w_down[0], norm_params[0]
    )
    second, kept_two = layer_forward(
        first_out, w_qkv[1], w_out[1], w_in[1], w_down[1], norm_params[1]
    )
    outputs = first_out + keep_rows * (second - first_out)
    masked_grad = cotangent * loss_mask.astype(jnp.float32)[:, None]
    grad_two, weights_two, norms_two = layer_backward(
        keep_rows * masked_grad, kept_two, w_qkv[1], w_out[1], w_in[1], w_down[1], norm_params[1]
    )
    blocks_two = tile_blocks(*weights_two)
    grad_first = (1.0 - keep_rows) * masked_grad + grad_two
    in_grads, weights_one, norms_one = layer_backward(
        grad_first, kept_one, w_qkv[0], w_out[0], w_in[0], w_down[0], norm_params[0]
    )
    blocks_one = tile_blocks(*weights_one)
    reduced = lax.psum_scatter(
        jnp.stack([blocks_one, blocks_two]), "dp", scatter_dimension=1, tiled=True
    )
    norm_grads = lax.psum(jnp.stack([norms_one, norms_two]), ("dp", "mp"))
    per_owner = reduced.shape[1]
    block_grads = reduced.reshape(-1, BLOCK, BLOCK)
    current = jnp.stack(
        [
            tile_blocks(w_qkv[0], w_out[0], w_in[0], w_down[0]),
            tile_blocks(w_qkv[1], w_out[1], w_in[1], w_down[1]),
        ]
    )
    owner_blocks = lax.dynamic_slice_in_dim(
        current, lax.axis_index("dp") * per_owner, per_owner, 1
    ).reshape(-1, BLOCK, BLOCK)
    left_new = stat_decay * left_stats + (1.0 - stat_decay) * jnp.einsum(
        "nij,nkj->nik", block_grads, block_grads, precision=HIGHEST
    )
    right_new = stat_decay * right_stats + (1.0 - stat_decay) * jnp.einsum(
        "nji,njk->nik", block_grads, block_grads, precision=HIGHEST
    )
    right_side = jnp.einsum("nij,njk->nik", block_grads, right_roots, precision=HIGHEST)
    precond = jnp.einsum("nij,njk->nik", left_roots, right_side, precision=HIGHEST)
    renewed = owner_blocks - shampoo_rate * precond * lax.rsqrt(
        jnp.mean(precond * precond, axis=(1, 2), keepdims=True) + graft_eps
    )
    everywhere = lax.all_gather(renewed.reshape(reduced.shape), "dp", axis=1, tiled=True)
    shape_list = [
        tuple(w_qkv.shape[1:]),
        tuple(w_out.shape[1:]),
        tuple(w_in.shape[1:]),
        tuple(w_down.shape[1:]),
    ]
    layer_one = untile_blocks(everywhere[0], shape_list)
    layer_two = untile_blocks(everywhere[1], shape_list)
    qkv_new = jnp.stack([layer_one[0], layer_two[0]])
    out_new = jnp.stack([layer_one[1], layer_two[1]])
    in_new = jnp.stack([layer_one[2], layer_two[2]])
    down_new = jnp.stack([layer_one[3], layer_two[3]])
    moments_new = moment_decay * norm_moments + (1.0 - moment_decay) * norm_grads * norm_grads
    norms_new = norm_params - vector_rate * norm_grads / (jnp.sqrt(moments_new) + vector_eps)
    return (
        outputs,
        in_grads,
        block_grads,
        left_new,
        right_new,
        qkv_new,
        out_new,
        in_new,
        down_new,
        norm_grads,
        moments_new,
        norms_new,
    )


def solution(mesh):
    in_specs = (
        P(("dp", "mp"), None),
        P(("dp", "mp"), None),
        P(("dp", "mp")),
        P("dp"),
        P(None, None, None, "mp"),
        P(None, "mp", None),
        P(None, None, "mp"),
        P(None, "mp", None),
        P(),
        P(),
        P(("dp", "mp"), None, None),
        P(("dp", "mp"), None, None),
        P(("dp", "mp"), None, None),
        P(("dp", "mp"), None, None),
    )
    out_specs = (
        P(("dp", "mp"), None),
        P(("dp", "mp"), None),
        P(("dp", "mp"), None, None),
        P(("dp", "mp"), None, None),
        P(("dp", "mp"), None, None),
        P(None, None, None, "mp"),
        P(None, "mp", None),
        P(None, None, "mp"),
        P(None, "mp", None),
        P(),
        P(),
        P(),
    )
    return jax.shard_map(
        on_device, mesh=mesh, in_specs=in_specs, out_specs=out_specs, check_vma=False
    )
```

profile of v0, /device:TPU:0, one launch (start us, length us, event | category | flops | bytes accessed | tf_op | source)
XLA Modules:
  0.0 1713.6 jit_solution(16556802029183090599)
XLA Ops:
  8.0 67.9 %all-gather.10.cloned.1.call-done = f32[1024,768]{1,0:T(8,128)} async-done(((f32[256,768]{1,0:T(8,128)}), f32[1024,768]{1,0:T(8,128)}) %all-gather.10.cloned.1.call-update) | async-done | bytes 3145744 | tf_op jit(solution)/shard_map/all_gather | solution.py:38
  115.1 59.0 %reduce-scatter.12.cloned.1.call-done = f32[256,768]{1,0:T(8,128)} async-done(((f32[1024,768]{1,0:T(8,128)}), f32[256,768]{1,0:T(8,128)}) %reduce-scatter.12.cloned.1.call-update) | async-done | bytes 786448 | tf_op jit(solution)/shard_map/reduce_scatter | solution.py:42
  177.4 63.6 %all-gather.12.cloned.1.call-done = f32[1024,768]{1,0:T(8,128)} async-done(((f32[256,768]{1,0:T(8,128)}), f32[1024,768]{1,0:T(8,128)}) %all-gather.12.cloned.1.call-update) | async-done | bytes 3145744 | tf_op jit(solution)/shard_map/all_gather | solution.py:38
  253.3 11.5 fusion.53
  264.9 59.0 %reduce-scatter.14.cloned.1.call-done = f32[256,768]{1,0:T(8,128)} async-done(((f32[1024,768]{1,0:T(8,128)}), f32[256,768]{1,0:T(8,128)}) %reduce-scatter.14.cloned.1.call-update) | async-done | bytes 786448 | tf_op jit(solution)/shard_map/reduce_scatter | solution.py:42
  331.2 59.4 %all-gather.14.cloned.1.call-done = f32[1024,768]{1,0:T(8,128)} async-done(((f32[256,768]{1,0:T(8,128)}), f32[1024,768]{1,0:T(8,128)}) %all-gather.14.cloned.1.call-update) | async-done | bytes 3145744 | tf_op jit(solution)/shard_map/all_gather | solution.py:38
  429.7 59.0 %reduce-scatter.16.cloned.1.call-done = f32[256,768]{1,0:T(8,128)} async-done(((f32[1024,768]{1,0:T(8,128)}), f32[256,768]{1,0:T(8,128)}) %reduce-scatter.16.cloned.1.call-update) | async-done | bytes 786448 | tf_op jit(solution)/shard_map/reduce_scatter | solution.py:42
  492.3 63.5 %all-gather.16.cloned.1.call-done = f32[1024,768]{1,0:T(8,128)} async-done(((f32[256,768]{1,0:T(8,128)}), f32[1024,768]{1,0:T(8,128)}) %all-gather.16.cloned.1.call-update) | async-done | bytes 3145744 | tf_op jit(solution)/shard_map/all_gather | solution.py:38
  568.0 11.6 fusion.45
  580.4 58.3 %reduce-scatter.18.cloned.1.call-done = f32[256,768]{1,0:T(8,128)} async-done(((f32[1024,768]{1,0:T(8,128)}), f32[256,768]{1,0:T(8,128)}) %reduce-scatter.18.cloned.1.call-update) | async-done | bytes 786448 | tf_op jit(solution)/shard_map/reduce_scatter | solution.py:42
  644.2 63.6 %all-gather.18.cloned.1.call-done = f32[1024,768]{1,0:T(8,128)} async-done(((f32[256,768]{1,0:T(8,128)}), f32[1024,768]{1,0:T(8,128)}) %all-gather.18.cloned.1.call-update) | async-done | bytes 3145744 | tf_op jit(solution)/shard_map/all_gather | solution.py:46
  707.8 11.8 fusion.26
  721.2 11.0 fusion.47
  732.3 59.0 %reduce-scatter.20.cloned.1.call-done = f32[256,768]{1,0:T(8,128)} async-done(((f32[1024,768]{1,0:T(8,128)}), f32[256,768]{1,0:T(8,128)}) %reduce-scatter.20.cloned.1.call-update) | async-done | bytes 786448 | tf_op jit(solution)/shard_map/reduce_scatter | solution.py:50
  797.7 61.2 %all-gather.20.cloned.1.call-done = f32[1024,768]{1,0:T(8,128)} async-done(((f32[256,768]{1,0:T(8,128)}), f32[1024,768]{1,0:T(8,128)}) %all-gather.20.cloned.1.call-update) | async-done | bytes 3145744 | tf_op jit(solution)/shard_map/all_gather | solution.py:46
  864.6 15.8 fusion.6
  880.4 15.7 multiply_multiply_fusion.1
  896.1 12.2 fusion.129
  927.6 58.8 %reduce-scatter.22.cloned.1.call-done = f32[256,768]{1,0:T(8,128)} async-done(((f32[1024,768]{1,0:T(8,128)}), f32[256,768]{1,0:T(8,128)}) %reduce-scatter.22.cloned.1.call-update) | async-done | bytes 786448 | tf_op jit(solution)/shard_map/reduce_scatter | solution.py:50
  990.4 63.6 %all-gather.22.cloned.1.call-done = f32[1024,768]{1,0:T(8,128)} async-done(((f32[256,768]{1,0:T(8,128)}), f32[1024,768]{1,0:T(8,128)}) %all-gather.22.cloned.1.call-update) | async-done | bytes 3145744 | tf_op jit(solution)/shard_map/all_gather | solution.py:46
  1054.1 11.4 fusion.31
  1067.0 11.0 fusion.55
  1078.2 59.0 %reduce-scatter.24.cloned.1.call-done = f32[256,768]{1,0:T(8,128)} async-done(((f32[1024,768]{1,0:T(8,128)}), f32[256,768]{1,0:T(8,128)}) %reduce-scatter.24.cloned.1.call-update) | async-done | bytes 786448 | tf_op jit(solution)/shard_map/reduce_scatter | solution.py:50
  1140.8 11.9 fusion.135
  1254.1 15.7 fusion.7
  1269.8 15.7 multiply_multiply_fusion
  1285.5 12.2 fusion.131
  1341.0 18.6 %reshape.400 = f32[192,18432]{1,0:T(8,128)} reshape(f32[192,2,96,96]{3,2,1,0:T(8,128)} %copy_bitcast_fusion) | data formatting | bytes 28311552
  1360.8 10.9 convolution_bitcast_fusion
  1441.3 11.2 maximum_bitcast_fusion.2
  1479.0 45.0 %psum.7 = f32[2,2,2,768]{3,2,1,0:T(2,128)S(1)} all-reduce(f32[2,2,2,768]{3,2,1,0:T(2,128)S(1)} %pad_maximum_fusion.15), channel_id=1, replica_groups=mesh['dp'=8,'mp'=4] {'dp','mp'}, use_global_device_ids=true, to_apply=%region_40.41 | all-reduce | flops 6144 | bytes 49152 | tf_op jit(solution)/shard_map/psum | solution.py:279
  1539.8 85.8 %all-gather.26.cloned.1.call-done = f32[2,192,96,96]{2,3,1,0:T(8,128)} async-done(((f32[2,24,96,96]{2,3,1,0:T(8,128)}), f32[2,192,96,96]{2,3,1,0:T(8,128)}) %all-gather.26.cloned.1.call-update) | async-done | bytes 14155792 | tf_op jit(solution)/shard_map/all_gather | solution.py:302
  (364 shorter events, 503.1 us)
Async XLA Ops:
  7.2 1464.5 %copy-start = (f32[48,96,96]{2,1,0:T(8,128)S(1)}, f32[48,96,96]{2,1,0:T(8,128)}, u32[]{:S(2)}) copy-start(f32[48,96,96]{2,1,0:T(8,128)} %param.26) | copy-start | bytes 5308420
  7.2 68.6 %all-gather.10.cloned.1.call-start = ((), (), s32[]{:S(2)}) async-start(), calls=%async_computation.9 | async-start | bytes 3932160 | tf_op jit(solution)/shard_map/all_gather | solution.py:38
  7.9 166.2 %reduce-scatter.12.cloned.1.call-start = ((), (), s32[]{:S(2)}) async-start(), calls=%async_computation.10 | async-start | bytes 3932160 | tf_op jit(solution)/shard_map/reduce_scatter | solution.py:42
  84.3 12.9 copy-start.46
  110.5 63.6 %copy-start.57 = (f32[256,768]{1,0:T(8,128)S(1)}, f32[256,768]{1,0:T(8,128)}, u32[]{:S(2)}) copy-start(f32[256,768]{1,0:T(8,128)} %param.14) | copy-start | bytes 2359300
  115.0 126.0 %all-gather.12.cloned.1.call-start = ((), (), s32[]{:S(2)}) async-start(), calls=%async_computation.11 | async-start | bytes 3932160 | tf_op jit(solution)/shard_map/all_gather | solution.py:38
  177.4 146.6 %reduce-scatter.14.cloned.1.call-start = ((), (), s32[]{:S(2)}) async-start(), calls=%async_computation.12 | async-start | bytes 3932160 | tf_op jit(solution)/shard_map/reduce_scatter | solution.py:42
  264.9 125.8 %all-gather.14.cloned.1.call-start = ((), (), s32[]{:S(2)}) async-start(), calls=%async_computation.13 | async-start | bytes 3932160 | tf_op jit(solution)/shard_map/all_gather | solution.py:38
  327.0 161.7 %reduce-scatter.16.cloned.1.call-start = ((), (), s32[]{:S(2)}) async-start(), calls=%async_computation.14 | async-start | bytes 3932160 | tf_op jit(solution)/shard_map/reduce_scatter | solution.py:42
  399.1 12.8 copy-start.48
  429.6 126.2 %all-gather.16.cloned.1.call-start = ((), (), s32[]{:S(2)}) async-start(), calls=%async_computation.15 | async-start | bytes 3932160 | tf_op jit(solution)/shard_map/all_gather | solution.py:38
  492.1 146.6 %reduce-scatter.18.cloned.1.call-start = ((), (), s32[]{:S(2)}) async-start(), calls=%async_computation.16 | async-start | bytes 3932160 | tf_op jit(solution)/shard_map/reduce_scatter | solution.py:42
  579.6 128.2 %all-gather.18.cloned.1.call-start = ((), (), s32[]{:S(2)}) async-start(), calls=%async_computation.17 | async-start | bytes 3932160 | tf_op jit(solution)/shard_map/all_gather | solution.py:46
  644.1 147.2 %reduce-scatter.20.cloned.1.call-start = ((), (), s32[]{:S(2)}) async-start(), calls=%async_computation.18 | async-start | bytes 3932160 | tf_op jit(solution)/shard_map/reduce_scatter | solution.py:50
  732.3 126.6 %all-gather.20.cloned.1.call-start = ((), (), s32[]{:S(2)}) async-start(), calls=%async_computation.19 | async-start | bytes 3932160 | tf_op jit(solution)/shard_map/all_gather | solution.py:46
  795.2 191.2 %reduce-scatter.22.cloned.1.call-start = ((), (), s32[]{:S(2)}) async-start(), calls=%async_computation.20 | async-start | bytes 3932160 | tf_op jit(solution)/shard_map/reduce_scatter | solution.py:50
  864.6 15.8 copy-start.49
  880.4 36.2 %copy-start.61 = (f32[3,64,1024]{2,1,0:T(8,128)}, f32[3,64,1024]{2,1,0:T(8,128)S(1)}, u32[]{:S(2)}) copy-start(f32[3,64,1024]{2,1,0:T(8,128)S(1)} %fusion.6) | copy-start | bytes 2359300
  880.4 15.7 copy-start.32
  927.4 126.7 %all-gather.22.cloned.1.call-start = ((), (), s32[]{:S(2)}) async-start(), calls=%async_computation.21 | async-start | bytes 3932160 | tf_op jit(solution)/shard_map/all_gather | solution.py:46
  990.4 146.8 %reduce-scatter.24.cloned.1.call-start = ((), (), s32[]{:S(2)}) async-start(), calls=%async_computation.22 | async-start | bytes 3932160 | tf_op jit(solution)/shard_map/reduce_scatter | solution.py:50
  1078.1 59.1 %copy-start.11 = (f32[256,768]{1,0:T(8,128)S(1)}, f32[256,768]{1,0:T(8,128)}, u32[]{:S(2)}) copy-start(f32[256,768]{1,0:T(8,128)} %copy-done.10) | copy-start | bytes 2359300
  1078.1 170.6 %all-gather.24.cloned.1.call-start = ((), (), s32[]{:S(2)}) async-start(), calls=%async_computation.23 | async-start | bytes 3932160 | tf_op jit(solution)/shard_map/all_gather | solution.py:46
  1140.8 319.7 %reduce-scatter.28.cloned.1.call-start = ((), (), s32[]{:S(2)}) async-start(), calls=%async_computation.26 | async-start | bytes 15925248
  1254.1 15.7 copy-start.47
  1269.8 36.1 %copy-start.63 = (f32[3,64,1024]{2,1,0:T(8,128)}, f32[3,64,1024]{2,1,0:T(8,128)S(1)}, u32[]{:S(2)}) copy-start(f32[3,64,1024]{2,1,0:T(8,128)S(1)} %fusion.7) | copy-start | bytes 2359300
  1269.8 15.7 copy-start.28
  1359.7 165.0 %reduce-scatter.26.cloned.1.call-start = ((), (), s32[]{:S(2)}) async-start(), calls=%async_computation.24 | async-start | bytes 3932160 | tf_op jit(solution)/shard_map/reduce_scatter | solution.py:50
  1371.7 253.9 %all-gather.26.cloned.1.call-start = ((), (), s32[]{:S(2)}) async-start(), calls=%async_computation.25 | async-start | bytes 21233664 | tf_op jit(solution)/shard_map/all_gather | solution.py:302
  1476.9 47.1 %copy-start.69 = (f32[2,2,2,768]{3,2,1,0:T(2,128)S(1)}, f32[2,2,2,768]{3,2,1,0:T(2,128)}, u32[]{:S(2)}) copy-start(f32[2,2,2,768]{3,2,1,0:T(2,128)} %param.22) | copy-start | bytes 73732
  1476.9 47.1 %copy-start.71 = (f32[2,2,2,768]{3,2,1,0:T(2,128)S(1)}, f32[2,2,2,768]{3,2,1,0:T(2,128)}, u32[]{:S(2)}) copy-start(f32[2,2,2,768]{3,2,1,0:T(2,128)} %param.23) | copy-start | bytes 73732
  1478.6 46.0 %copy-start.37 = (f32[256,768]{1,0:T(8,128)S(1)}, f32[256,768]{1,0:T(8,128)}, u32[]{:S(2)}) copy-start(f32[256,768]{1,0:T(8,128)} %subtract_multiply_fusion) | copy-start | bytes 2359300
  (70 other events, 322.7 us)
Sparse Core Ops, SparseCore 0:
  9.6 66.1 all-gather.9
  115.2 58.8 reduce-scatter.11
  177.5 63.5 all-gather.11
  265.0 58.8 reduce-scatter.13
  327.1 63.5 all-gather.13
  429.7 58.8 reduce-scatter.15
  492.2 63.5 all-gather.15
  579.8 58.8 reduce-scatter.17
  644.2 63.5 all-gather.17
  732.4 58.8 reduce-scatter.19
  795.4 63.5 all-gather.19
  927.5 58.8 reduce-scatter.21
  990.5 63.5 all-gather.21
  1078.2 58.8 reduce-scatter.23
  1140.9 63.5 all-gather.23
  1359.8 100.6 reduce-scatter.27
  1463.2 61.2 reduce-scatter.25
  1526.9 98.7 all-gather.25
where the time goes:
time: 1720 us; the launch traced here: 1710 us
  waiting for transfers between devices  947 us (55%)
  matrix products  380 us (22%)
  local copies, waits for them, and re-layouts  246 us (14%)
  other arithmetic  78.5 us (5%)
  blocking collectives  45 us (3%)
    all_gather x4, waiting for transfers between devices, gather_rows(): return lax.all_gather(local_rows, 'mp', axis=0, tiled=True)  254 us
    reduce_scatter x4, waiting for transfers between devices, reduce_rows(): lax.psum_scatter(partial_value, 'mp', scatter_dimension=0, tiled=True)  235 us
    all_gather x4, waiting for transfers between devices, gather_grads(): return lax.all_gather(local_rows, 'mp', axis=0, tiled=True)  188 us
    reduce_scatter x4, waiting for transfers between devices, reduce_grads(): lax.psum_scatter(partial_value, 'mp', scatter_dimension=0, tiled=True)  177 us
    all_gather x1, waiting for transfers between devices, on_device(): lax.all_gather(renewed.reshape(reduced.shape), 'dp', axis=1, tiled=True)  85.8 us
    dot_general x6, matrix products, matmul_t(): return jnp.einsum('sa,ba->sb', left_op, right_op, precision=HIGHEST)  56.3 us
    dot_general x6, matrix products, matmul(): return jnp.dot(left_op, right_op, precision=HIGHEST)  53.2 us
    dot_general x6, matrix products, inner_rows(): return jnp.einsum('sa,sb->ab', left_op, right_op, precision=HIGHEST)  51.9 us
  transfers between devices with their start and end apart: 18, of which 16 were waited for; matrix products, arithmetic and copies ran while one was open for 14% of the time, Pallas kernels for 0%

commit v1 on v0

--- a/solution.py
+++ b/solution.py
@@ -1,9 +1,12 @@
+import functools
 import math
 
 import jax
 import jax.numpy as jnp
 from jax import lax
-from jax.sharding import PartitionSpec as P
+from jax.experimental import pallas as pl
+from jax.experimental.pallas import tpu as pltpu
+from jax.sharding import Mesh, PartitionSpec as P
 
 HEAD = 64
 LEN = 1024
@@ -330,7 +333,1214 @@
     )
 
 
+HIGH = lax.Precision.HIGH
+FINE = ("e", "c", "mh", "ml")
+FLIP = [(0, 1), (1, 0)]
+MESH_ID = pl.DeviceIdType.MESH
+NN = (((1,), (0,)), ((), ()))
+NT = (((1,), (1,)), ((), ()))
+TN = (((0,), (0,)), ((), ()))
+F32 = jnp.float32
+BF16 = jnp.bfloat16
+VMEM_BYTES = 60 * 2**20
+
+
+def dot(left_op, right_op, dims):
+    return lax.dot_general(left_op, right_op, dims, precision=HIGH, preferred_element_type=F32)
+
+
+def dot16(left_op, right_op, dims):
+    return lax.dot_general(left_op, right_op, dims, preferred_element_type=F32)
+
+
+def halves(value):
+    high = value.astype(BF16)
+    return high, (value - high.astype(F32)).astype(BF16)
+
+
+class Pair:
+    def __init__(self, full, part, core_in, chip_in, send, recv):
+        self.full, self.part, self.core_in, self.chip_in = full, part, core_in, chip_in
+        self.send, self.recv = send, recv
+        self.rows = full.shape[0] // 4
+        self.half = self.rows // 2
+        self.core = {"c": 1 - lax.axis_index("c")}
+        self.chip = {"ml": 1 - lax.axis_index("ml")}
+        r, h = self.rows, self.half
+        self.z = [self._copy(full, i * h, full, 2 * r + i * r, h, i, self.chip) for i in range(2)]
+        self.own = self._copy(full, 0, full, r, r, 2, self.core)
+        self.fwd = [
+            self._copy(full, 2 * r + i * r, full, 2 * r + i * r + h, h, 3 + i, self.core) for i in range(2)
+        ]
+        self.back = self._copy(part, r, core_in, 0, r, 5, self.core)
+        self.side = [
+            self._copy(part, 2 * r + i * r + h, core_in, r + i * h, h, 6 + i, self.core) for i in range(2)
+        ]
+        self.home = [self._copy(part, 2 * r + i * r, chip_in, i * h, h, 8 + i, self.chip) for i in range(2)]
+
+    def _copy(self, src, src_row, dst, dst_row, count, slot, device):
+        return pltpu.make_async_remote_copy(
+            src_ref=src.at[pl.ds(src_row, count)],
+            dst_ref=dst.at[pl.ds(dst_row, count)],
+            send_sem=self.send.at[slot],
+            recv_sem=self.recv.at[slot],
+            device_id=device,
+            device_id_type=MESH_ID,
+        )
+
+    def devices(self):
+        return [self.core, self.chip]
+
+    def start(self):
+        for copy in (self.z[0], self.own, self.z[1]):
+            copy.start()
+
+    def arrive(self, tile):
+        if tile == 1:
+            self.own.wait_recv()
+        elif tile >= 2:
+            self.z[tile - 2].wait_recv()
+            self.fwd[tile - 2].start()
+            self.fwd[tile - 2].wait_recv()
+
+    def reduce(self, tile):
+        if tile == 1:
+            self.back.start()
+        elif tile >= 2:
+            i, r, h = tile - 2, self.rows, self.half
+            self.side[i].start()
+            self.side[i].wait_recv()
+            mine = pl.ds(2 * r + i * r, h)
+            self.part[mine] = self.part[mine] + self.core_in[pl.ds(r + i * h, h)]
+            self.home[i].start()
+
+    def finish(self):
+        self.back.wait_recv()
+        for copy in self.home:
+            copy.wait_recv()
+        for copy in (*self.z, self.own, *self.fwd, self.back, *self.side, *self.home):
+            copy.wait_send()
+
+    def total(self):
+        r = self.rows
+        return self.part[:r] + self.core_in[:r] + self.chip_in[...]
+
+
+PAIR_SLOTS = 10
+
+
+def beside(e, mask):
+    y, x = e // 2, e % 2
+    return 2 * (1 - y if mask >= 2 else y) + (1 - x if mask % 2 else x)
+
+
+def is_away():
+    return lax.axis_index("c") != lax.axis_index("mh")
+
+
+def partner_id():
+    return {"c": 1 - lax.axis_index("c"), "mh": 1 - lax.axis_index("mh")}
+
+
+class Fetch:
+    def __init__(self, owned, foreign, send, recv):
+        self.owned, self.foreign, self.send, self.recv = owned, foreign, send, recv
+        self.e = lax.axis_index("e")
+        self.near = [{"e": beside(self.e, mask)} for mask in (1, 2, 3)]
+
+    def _piece(self, ref):
+        count = ref.shape[-2] // 4
+        rows = pl.ds(pl.multiple_of(self.e * count, count), count)
+        return ref.at[:, rows] if len(ref.shape) == 3 else ref.at[rows]
+
+    def _copy(self, job, hop):
+        target = self._piece(self.foreign[job])
+        return pltpu.make_async_remote_copy(
+            src_ref=self._piece(self.owned[job]) if hop == 0 else target,
+            dst_ref=target,
+            send_sem=self.send.at[4 * job + hop],
+            recv_sem=self.recv.at[4 * job + hop],
+            device_id=partner_id() if hop == 0 else self.near[hop - 1],
+            device_id_type=MESH_ID,
+        )
+
+    def devices(self):
+        return [partner_id(), *self.near]
+
+    def cross(self):
+        @pl.when(is_away())
+        def _():
+            for job in range(len(self.owned)):
+                self._copy(job, 0).start()
+
+    def spread(self, job):
+        @pl.when(is_away())
+        def _():
+            self._copy(job, 0).wait_recv()
+            for hop in (1, 2, 3):
+                self._copy(job, hop).start()
+
+    def finish(self):
+        @pl.when(is_away())
+        def _():
+            for job in range(len(self.owned)):
+                for hop in (1, 2, 3):
+                    self._copy(job, hop).wait_recv()
+                for hop in range(4):
+                    self._copy(job, hop).wait_send()
+
+
+class Swap:
+    def __init__(self, sources, targets, send, recv, first):
+        self.sources, self.targets, self.send, self.recv, self.first = sources, targets, send, recv, first
+
+    def _away(self, i):
+        return pltpu.make_async_remote_copy(
+            src_ref=self.sources[i],
+            dst_ref=self.targets[i],
+            send_sem=self.send.at[self.first + i],
+            recv_sem=self.recv.at[self.first + i],
+            device_id=partner_id(),
+            device_id_type=MESH_ID,
+        )
+
+    def _here(self, i):
+        return pltpu.make_async_copy(self.sources[i], self.targets[i], self.send.at[self.first + i])
+
+    def start(self):
+        for i in range(len(self.sources)):
+            pl.when(is_away())(lambda: self._away(i).start())
+            pl.when(jnp.logical_not(is_away()))(lambda: self._here(i).start())
+
+    def finish(self):
+        for i in range(len(self.sources)):
+            pl.when(is_away())(lambda: self._away(i).wait())
+            pl.when(jnp.logical_not(is_away()))(lambda: self._here(i).wait())
+
+
+def chosen(order, e):
+    value = order[0]
+    for i in range(1, len(order)):
+        value = jnp.where(e == i, order[i], value)
+    return value
+
+
+ATT_ORDER, ATT_CHIP, ATT_UNIT = (0, 3, 1, 2), (0, 2, 3, 1), 0
+FFN_ORDER, FFN_CHIP, FFN_UNIT = (2, 0, 1, 3), (1, 2, 0, 3), 8
+UNITS = 3
+
+
+class PlaneSum:
+    def __init__(self, grads, got, order, send, recv):
+        self.grads, self.got, self.order, self.send, self.recv = grads, got, order, send, recv
+        self.e = lax.axis_index("e")
+        self.count = got.shape[1]
+        self.copies = [self._copy(mask) for mask in (1, 2, 3)]
+
+    def _copy(self, mask):
+        there = beside(self.e, mask)
+        rows = pl.ds(pl.multiple_of(chosen(self.order, there) * self.count, self.count), self.count)
+        return pltpu.make_async_remote_copy(
+            src_ref=self.grads.at[rows],
+            dst_ref=self.got.at[mask - 1],
+            send_sem=self.send.at[mask - 1],
+            recv_sem=self.recv.at[mask - 1],
+            device_id={"e": there},
+            device_id_type=MESH_ID,
+        )
+
+    def start(self):
+        for copy in self.copies:
+            copy.start()
+
+    def finish(self):
+        for copy in self.copies:
+            copy.wait()
+
+
+class OwnerSend:
+    def __init__(self, grads, got, acc, owned, order, chip, unit, send, recv, loads):
+        self.acc, self.owned, self.chip, self.unit = acc, owned, chip, unit
+        self.send, self.recv, self.loads = send, recv, loads
+        self.e, self.c, self.mh = lax.axis_index("e"), lax.axis_index("c"), lax.axis_index("mh")
+        self.count = got.shape[1]
+        self.per = self.count // BLOCK
+        piece = chosen(order, self.e)
+        rows = pl.ds(pl.multiple_of(piece * self.count, self.count), self.count)
+        self.first = unit + piece * self.per
+        sources = [grads.at[rows]] + [got.at[i] for i in range(3)]
+        self.reads = [pltpu.make_async_copy(sources[i], acc.at[i], loads.at[i]) for i in range(4)]
+
+    def begin(self):
+        for read in self.reads:
+            read.start()
+
+    def _unit(self, k):
+        b = self.first + k
+        e, c, slot = b // (2 * UNITS), (b // UNITS) % 2, b % UNITS
+        here = jnp.logical_and(jnp.logical_and(e == self.e, c == self.c), self.c == self.mh)
+        source = self.acc.at[0, pl.ds(k * BLOCK, BLOCK)]
+        target = self.owned.at[self.mh, pl.ds(pl.multiple_of(slot * BLOCK, BLOCK), BLOCK)]
+        remote = pltpu.make_async_remote_copy(
+            src_ref=source,
+            dst_ref=target,
+            send_sem=self.send.at[k],
+            recv_sem=self.recv.at[self.mh * UNITS + slot],
+            device_id={"e": e, "c": c, "mh": self.c},
+            device_id_type=MESH_ID,
+        )
+        return here, remote, pltpu.make_async_copy(source, target, self.send.at[k])
+
+    def ship(self):
+        for read in self.reads:
+            read.wait()
+        self.acc[0] = self.acc[0] + self.acc[1] + self.acc[2] + self.acc[3]
+        for k in range(self.per):
+            here, remote, local = self._unit(k)
+            pl.when(here)(local.start)
+            pl.when(jnp.logical_not(here))(remote.start)
+
+    def finish(self):
+        for k in range(self.per):
+            here, remote, local = self._unit(k)
+            pl.when(here)(local.wait)
+            pl.when(jnp.logical_not(here))(remote.wait_send)
+        first = UNITS * (2 * self.e + self.c)
+        for mh in range(2):
+            for slot in range(UNITS):
+                b = first + slot
+                mine = b >= FFN_UNIT if self.unit == FFN_UNIT else b < FFN_UNIT
+                origin = chosen(self.chip, (b - self.unit) // self.per)
+                here = jnp.logical_and(origin == self.e, jnp.logical_and(self.mh == self.c, self.mh == mh))
+                piece = self.owned.at[mh, pl.ds(slot * BLOCK, BLOCK)]
+                wait = pltpu.make_async_remote_copy(
+                    src_ref=piece,
+                    dst_ref=piece,
+                    send_sem=self.send.at[0],
+                    recv_sem=self.recv.at[mh * UNITS + slot],
+                    device_id={"c": 1 - self.c},
+                    device_id_type=MESH_ID,
+                )
+                pl.when(jnp.logical_and(mine, jnp.logical_not(here)))(wait.wait_recv)
+
+
+def near_chips():
+    return [{"e": beside(lax.axis_index("e"), mask)} for mask in (1, 2, 3)]
+
+
+def sixteen():
+    e, c, mh = (lax.axis_index(axis) for axis in ("e", "c", "mh"))
+    devices = []
+    for mask in range(4):
+        for flip_c in range(2):
+            for flip_h in range(2):
+                if mask or flip_c or flip_h:
+                    devices.append(
+                        {"e": beside(e, mask), "c": 1 - c if flip_c else c, "mh": 1 - mh if flip_h else mh}
+                    )
+    return devices
+
+
+class PlaneGather:
+    def __init__(self, rows, whole, send, recv, sem):
+        self.rows, self.whole, self.send, self.recv = rows, whole, send, recv
+        self.e, self.c = lax.axis_index("e"), lax.axis_index("c")
+        self.count = rows.shape[0]
+        self.half = rows.shape[1] // 2
+        self.local = pltpu.make_async_copy(rows, self._at(0, self.c), sem)
+        half = self.half
+        self.first = [self._copy(rows.at[:, pl.ds(i * half, half)], self._at(0, self.c, i), i, i + 1) for i in range(2)]
+        self.second = []
+        for i in range(2):
+            near, far = i + 1, 2 - i
+            self.second.append(self._copy(rows.at[:, pl.ds(i * half, half)], self._at(0, self.c, i), 2 + 2 * i, far))
+            place = self._at(near, self.c, i)
+            self.second.append(self._copy(place, place, 3 + 2 * i, far))
+        self.core = []
+        for mask in range(4):
+            place = self._at(mask, self.c)
+            self.core.append(self._copy(rows if mask == 0 else place, place, 6 + mask, 0))
+
+    def _at(self, mask, c, part=None):
+        owner = 2 * beside(self.e, mask) + c
+        span = pl.ds(pl.multiple_of(owner * self.count, self.count), self.count)
+        return self.whole.at[span] if part is None else self.whole.at[span, pl.ds(part * self.half, self.half)]
+
+    def _copy(self, source, target, slot, mask):
+        return pltpu.make_async_remote_copy(
+            src_ref=source,
+            dst_ref=target,
+            send_sem=self.send.at[slot],
+            recv_sem=self.recv.at[slot],
+            device_id={"e": beside(self.e, mask)} if mask else {"c": 1 - self.c},
+            device_id_type=MESH_ID,
+        )
+
+    def start(self):
+        self.local.start()
+        for copy in (*self.first, self.second[0], self.second[2], self.core[0]):
+            copy.start()
+
+    def middle(self):
+        for i in range(2):
+            self.first[i].wait_recv()
+            self.second[2 * i + 1].start()
+
+    def finish(self):
+        for i in range(2):
+            self.second[2 * i].wait_recv()
+        self.second[1].wait_recv()
+        self.second[3].wait_recv()
+        for mask in (1, 2, 3):
+            self.core[mask].start()
+        self.local.wait()
+        for copy in self.core:
+            copy.wait_recv()
+        for copy in (*self.first, *self.second, *self.core):
+            copy.wait_send()
+
+
+def greet(always, if_away):
+    barrier = pltpu.get_barrier_semaphore()
+
+    def signal(devices):
+        for device in devices:
+            pl.semaphore_signal(barrier, inc=1, device_id=device, device_id_type=MESH_ID)
+
+    signal(always)
+
+    @pl.when(is_away())
+    def _():
+        signal(if_away)
+        pl.semaphore_wait(barrier, len(always) + len(if_away))
+
+    if always:
+
+        @pl.when(jnp.logical_not(is_away()))
+        def _():
+            pl.semaphore_wait(barrier, len(always))
+
+
+def load_quarter(owned, foreign, target, sem):
+    pl.when(is_away())(lambda: pltpu.make_async_copy(foreign, target, sem).start())
+    pl.when(jnp.logical_not(is_away()))(lambda: pltpu.make_async_copy(owned, target, sem).start())
+    return pltpu.make_async_copy(owned, target, sem)
+
+
+def move_scratch(count):
+    return [pltpu.SemaphoreType.DMA((count,)), pltpu.SemaphoreType.DMA((count,))]
+
+
+def own_scratch(rows, width):
+    return move_scratch(3) + [
+        pltpu.SemaphoreType.DMA((4,)), pltpu.SemaphoreType.DMA((2 * UNITS,)), pltpu.SemaphoreType.DMA((4,)),
+        pltpu.VMEM((4, rows, width), F32),
+    ]
+
+
+def pair_scratch(rows, width):
+    return [
+        pltpu.VMEM((4 * rows, width), F32),
+        pltpu.VMEM((4 * rows, width), F32),
+        pltpu.VMEM((2 * rows, width), F32),
+        pltpu.VMEM((rows, width), F32),
+        pltpu.SemaphoreType.DMA((PAIR_SLOTS,)),
+        pltpu.SemaphoreType.DMA((PAIR_SLOTS,)),
+    ]
+
+
+VM = pl.BlockSpec(memory_space=pltpu.VMEM)
+HB = pl.BlockSpec(memory_space=pl.ANY)
+
+
+def shape(*dims):
+    return jax.ShapeDtypeStruct(dims, F32)
+
+
+def fetch(sources, targets, sems, first=0):
+    copies = []
+    for i, (source, target) in enumerate(zip(sources, targets)):
+        copies.append(pltpu.make_async_copy(source, target, sems.at[first + i]))
+        copies[-1].start()
+    return copies
+
+
+def tile_rows(tile, rows):
+    return pl.ds(tile * rows, rows)
+
+
+def ln_out(value, norm_ref, result, normed_ref, scale_ref):
+    out, normed, scale = norm_forward(value, norm_ref[0:1], norm_ref[1:2])
+    result[...] = out
+    normed_ref[...] = normed
+    scale_ref[...] = jnp.broadcast_to(scale, scale_ref.shape)
+
+
+def open_kernel(rows_hbm, qkv_hbm, out_hbm, own_hbm, f_qkv, f_out, send, recv):
+    job = Fetch((qkv_hbm.at[0], out_hbm.at[0]), (f_qkv, f_out), send, recv)
+    swap = Swap((rows_hbm,), (own_hbm,), send, recv, 8)
+    greet([], job.devices())
+    job.cross()
+    swap.start()
+    job.spread(0)
+    job.spread(1)
+    swap.finish()
+    job.finish()
+
+
+def open_step(rows, w_qkv, w_out, collective):
+    return pl.pallas_call(
+        open_kernel,
+        out_shape=(shape(*rows.shape), shape(*w_qkv.shape[1:]), shape(*w_out.shape[1:])),
+        in_specs=[HB] * 3,
+        out_specs=(HB,) * 3,
+        scratch_shapes=move_scratch(9),
+        compiler_params=pltpu.CompilerParams(collective_id=collective, has_side_effects=True),
+        name="open_step",
+    )(rows, w_qkv, w_out)
+
+
+def ffn_fwd_kernel(
+    layer, last,
+    own_ref, norm_ref, in_hbm, down_hbm, f_in, f_down, extra_a, extra_b,
+    result, normed_ref, scale_ref, full_hbm, pre_hbm, cdf_hbm, got_a, got_b,
+    full, part, core_in, chip_in, send, recv, w_in, w_down, pre, cdf, sems, move_send, move_recv,
+):
+    pair = Pair(full, part, core_in, chip_in, send, recv)
+    rows = pair.rows
+    if last:
+        job = Swap((extra_a, extra_b), (got_a, got_b), move_send, move_recv, 0)
+        others = [partner_id()]
+    else:
+        job = Fetch((extra_a.at[layer + 1], extra_b.at[layer + 1]), (got_a, got_b), move_send, move_recv)
+        others = job.devices()
+    loads = [
+        load_quarter(in_hbm.at[layer], f_in, w_in, sems.at[0]),
+        load_quarter(down_hbm.at[layer], f_down, w_down, sems.at[1]),
+    ]
+    full[:rows] = own_ref[...]
+    greet(pair.devices(), others)
+    pair.start()
+    if last:
+        job.start()
+    else:
+        job.cross()
+    loads[0].wait()
+    stores = []
+    for tile in range(4):
+        span = tile_rows(tile, rows)
+        pair.arrive(tile)
+        if tile >= 2 and not last:
+            job.spread(tile - 2)
+        pre_act = dot(full[span], w_in[...], NN)
+        if tile == 0:
+            loads[1].wait()
+        gate = 0.5 * (1.0 + lax.erf(pre_act * sqrt_half))
+        pre[span] = pre_act
+        cdf[span] = gate
+        part[span] = dot(pre_act * gate, w_down[...], NN)
+        pair.reduce(tile)
+        stores += fetch(
+            (full.at[span], pre.at[span], cdf.at[span]),
+            (full_hbm.at[span], pre_hbm.at[span], cdf_hbm.at[span]),
+            sems,
+            2 + 3 * tile,
+        )
+    pair.finish()
+    ln_out(own_ref[...] + pair.total(), norm_ref, result, normed_ref, scale_ref)
+    job.finish()
+    for copy in stores:
+        copy.wait()
+
+
+def ffn_fwd(own, w_in, w_down, f_in, f_down, extra, norm, layer, last):
+    rows, width = own.shape
+    hidden = w_in.shape[2]
+    got = [shape(*(v.shape if last else v.shape[1:])) for v in extra]
+    result, normed, scale, full, pre, cdf, *got = pl.pallas_call(
+        functools.partial(ffn_fwd_kernel, layer, last),
+        out_shape=(
+            shape(rows, width), shape(rows, width), shape(rows, 128),
+            shape(4 * rows, width), shape(4 * rows, hidden), shape(4 * rows, hidden), *got,
+        ),
+        in_specs=[VM, VM] + [HB] * 6,
+        out_specs=(VM, VM, VM, HB, HB, HB, HB, HB),
+        scratch_shapes=pair_scratch(rows, width) + [
+            pltpu.VMEM(w_in.shape[1:], F32), pltpu.VMEM(w_down.shape[1:], F32),
+            pltpu.VMEM((4 * rows, hidden), F32), pltpu.VMEM((4 * rows, hidden), F32),
+            pltpu.SemaphoreType.DMA((14,)),
+        ] + move_scratch(8),
+        compiler_params=pltpu.CompilerParams(
+            collective_id=4 * layer + 1, has_side_effects=True, vmem_limit_bytes=VMEM_BYTES
+        ),
+        name="ffn_fwd",
+    )(own, norm, w_in, w_down, f_in, f_down, *extra)
+    return result, (full, pre, cdf, normed, scale), got
+
+
+def ln_back(grad, normed_ref, scale_ref, norm_ref, norm_grad):
+    normed = normed_ref[...]
+    norm_grad[0:1] = jnp.sum(grad * normed, axis=0, keepdims=True)
+    norm_grad[1:2] = jnp.sum(grad, axis=0, keepdims=True)
+    return norm_backward(grad, normed, scale_ref[:, :1], norm_ref[0:1])
+
+
+def ffn_bwd_kernel(
+    layer,
+    grad_ref, normed_ref, scale_ref, norm_ref, in_hbm, down_hbm, f_in, f_down, full_hbm, pre_hbm, cdf_hbm, *rest
+):
+    if layer == 0:
+        sum_hbm, own_hbm, part_hbm, *rest = rest
+    grad_own, norm_grad, grads_hbm, *rest = rest
+    if layer == 0:
+        got_hbm, owned_hbm, *rest = rest
+    full, part, core_in, chip_in, send, recv, w_in, w_down, mid, pre, cdf, grads, sems, *rest = rest
+    if layer == 0:
+        move_send, move_recv, own_send, own_recv, own_load, acc = rest
+    pair = Pair(full, part, core_in, chip_in, send, recv)
+    rows = pair.rows
+    hidden = w_in.shape[1]
+    loads = fetch((pre_hbm, cdf_hbm, full_hbm), (pre, cdf, mid), sems)
+    loads.append(load_quarter(down_hbm.at[layer], f_down, w_down, sems.at[3]))
+    loads.append(load_quarter(in_hbm.at[layer], f_in, w_in, sems.at[4]))
+    full[:rows] = ln_back(grad_ref[...], normed_ref, scale_ref, norm_ref, norm_grad)
+    if layer == 0:
+        job = PlaneSum(sum_hbm, got_hbm, ATT_ORDER, move_send, move_recv)
+        ship = OwnerSend(
+            own_hbm, part_hbm, acc, owned_hbm, FFN_ORDER, FFN_CHIP, FFN_UNIT, own_send, own_recv, own_load
+        )
+        ship.begin()
+    greet([pair.chip, *(sixteen() if layer == 0 else [pair.core])], [])
+    pair.start()
+    if layer == 0:
+        job.start()
+        ship.ship()
+    for copy in loads:
+        copy.wait()
+    for tile in range(4):
+        span = tile_rows(tile, rows)
+        pair.arrive(tile)
+        grad_act = dot(full[span], w_down[...], NT)
+        pre_act, gate = pre[span], cdf[span]
+        grad_pre = grad_act * (gate + pre_act * jnp.exp(-0.5 * pre_act * pre_act) * inv_sqrt_tau)
+        cdf[span] = pre_act * gate
+        pre[span] = grad_pre
+        part[span] = dot(grad_pre, w_in[...], NT)
+        pair.reduce(tile)
+    width = full.shape[1]
+
+    @pl.loop(0, width // 256)
+    def _(i):
+        cols = pl.ds(pl.multiple_of(i * 256, 256), 256)
+        grads[cols, :] = dot(mid[:, cols], pre[...], TN)
+
+    @pl.loop(0, hidden // 256)
+    def _(i):
+        cols = pl.ds(pl.multiple_of(i * 256, 256), 256)
+        target = pl.ds(pl.multiple_of(width + i * 256, 256), 256)
+        grads[target, :] = dot(cdf[:, cols], full[...], TN)
+
+    store = fetch((grads,), (grads_hbm,), sems, 5)[0]
+    pair.finish()
+    grad_own[...] = full[:rows] + pair.total()
+    store.wait()
+    if layer == 0:
+        job.finish()
+        ship.finish()
+
+
+def to_sum_args(to_sum, to_own):
+    return () if to_sum is None else (to_sum, *to_own)
+
+
+def ffn_bwd(grad, kept, w_in, w_down, f_in, f_down, to_sum, to_own, norm, layer):
+    full, pre, cdf, normed, scale = kept
+    rows, width = grad.shape
+    hidden = w_in.shape[2]
+    return pl.pallas_call(
+        functools.partial(ffn_bwd_kernel, layer),
+        out_shape=(
+            shape(rows, width), shape(2, width), shape(width + hidden, width),
+            *([shape(3, to_sum.shape[0] // 4, width), shape(2, UNITS * BLOCK, width)] if layer == 0 else []),
+        ),
+        in_specs=[VM] * 4 + [HB] * (7 if layer else 10),
+        out_specs=(VM, VM, HB) + (HB, HB) * (1 - layer),
+        scratch_shapes=pair_scratch(rows, width) + [
+            pltpu.VMEM(w_in.shape[1:], F32), pltpu.VMEM(w_down.shape[1:], F32),
+            pltpu.VMEM((4 * rows, width), F32),
+            pltpu.VMEM((4 * rows, hidden), F32), pltpu.VMEM((4 * rows, hidden), F32),
+            pltpu.VMEM((width + hidden, width), F32),
+            pltpu.SemaphoreType.DMA((6,)),
+        ] + (own_scratch((width + hidden) // 4, width) if layer == 0 else []),
+        compiler_params=pltpu.CompilerParams(
+            collective_id=4 * layer + 2, has_side_effects=True, vmem_limit_bytes=VMEM_BYTES
+        ),
+        name="ffn_bwd",
+    )(grad, normed, scale, norm, w_in, w_down, f_in, f_down, full, pre, cdf, *to_sum_args(to_sum, to_own))
+
+
+def attend_fwd_kernel(
+    layer,
+    own_ref, norm_ref, qkv_hbm, out_hbm, f_qkv, f_out, in_hbm, down_hbm,
+    result, normed_ref, scale_ref, full_hbm, proj_hbm, ctx_hbm, lse_hbm, f_in, f_down,
+    full, part, core_in, chip_in, send, recv, w_qkv, w_out, proj, ctx, lse, keys, values, sems, move_send, move_recv,
+):
+    pair = Pair(full, part, core_in, chip_in, send, recv)
+    rows = pair.rows
+    heads = w_out.shape[0] // HEAD
+    job = Fetch((in_hbm.at[layer], down_hbm.at[layer]), (f_in, f_down), move_send, move_recv)
+    loads = [
+        load_quarter(qkv_hbm.at[layer], f_qkv, w_qkv, sems.at[0]),
+        load_quarter(out_hbm.at[layer], f_out, w_out, sems.at[1]),
+    ]
+    full[:rows] = own_ref[...]
+    greet(pair.devices(), job.devices())
+    pair.start()
+    job.cross()
+    loads[0].wait()
+    stores = []
+    for tile in range(4):
+        span = tile_rows(tile, rows)
+        pair.arrive(tile)
+        for part_id in range(3):
+            proj[part_id, span] = dot(full[span], w_qkv[part_id], NT)
+        for head in range(heads):
+            cols = slice(head * HEAD, (head + 1) * HEAD)
+            high, low = halves(proj[1, span, cols])
+            keys[head, span] = jnp.concatenate([high, low, high], axis=1)
+            high, low = halves(proj[2, span, cols])
+            values[head, span] = jnp.concatenate([high, low], axis=1)
+        stores += fetch((full.at[span],), (full_hbm.at[span],), sems, 2 + tile)
+    stores += fetch((proj,), (proj_hbm,), sems, 6)
+    job.spread(0)
+    loads[1].wait()
+    lanes = lax.broadcasted_iota(jnp.int32, (rows, 128), 1)
+    for tile in (2, 3, 1, 0):
+        span = tile_rows(tile, rows)
+        sums = jnp.zeros((rows, 128), F32)
+        for head in range(heads):
+            cols = slice(head * HEAD, (head + 1) * HEAD)
+            high, low = halves(proj[0, span, cols] * (HEAD ** -0.5))
+            scores = dot16(jnp.concatenate([high, high, low], axis=1), keys[head], NT)
+            peak = jnp.max(scores, axis=1, keepdims=True)
+            exps = jnp.exp(scores - peak)
+            totals = jnp.sum(exps, axis=1, keepdims=True)
+            high, low = halves(exps)
+            mixed = dot16(high, values[head], NN)
+            rest = dot16(low, values[head, :, :HEAD], NN)
+            ctx[span, cols] = (mixed[:, :HEAD] + mixed[:, HEAD:] + rest) / totals
+            sums = jnp.where(lanes == head, peak + jnp.log(totals), sums)
+        lse[span] = sums
+        part[span] = dot(ctx[span], w_out[...], NN)
+        pair.reduce(tile)
+        if tile == 3:
+            job.spread(1)
+    stores += fetch((ctx, lse), (ctx_hbm, lse_hbm), sems, 7)
+    pair.finish()
+    ln_out(own_ref[...] + pair.total(), norm_ref, result, normed_ref, scale_ref)
+    job.finish()
+    for copy in stores:
+        copy.wait()
+
+
+def attend_fwd(own, w_qkv, w_out, f_qkv, f_out, w_in, w_down, norm, layer):
+    rows, width = own.shape
+    inner = w_out.shape[1]
+    heads = inner // HEAD
+    result, normed, scale, full, proj, ctx, lse, f_in, f_down = pl.pallas_call(
+        functools.partial(attend_fwd_kernel, layer),
+        out_shape=(
+            shape(rows, width), shape(rows, width), shape(rows, 128),
+            shape(4 * rows, width), shape(3, 4 * rows, inner), shape(4 * rows, inner), shape(4 * rows, 128),
+            shape(*w_in.shape[1:]), shape(*w_down.shape[1:]),
+        ),
+        in_specs=[VM, VM] + [HB] * 6,
+        out_specs=(VM, VM, VM) + (HB,) * 6,
+        scratch_shapes=pair_scratch(rows, width) + [
+            pltpu.VMEM(w_qkv.shape[1:], F32), pltpu.VMEM(w_out.shape[1:], F32),
+            pltpu.VMEM((3, 4 * rows, inner), F32), pltpu.VMEM((4 * rows, inner), F32),
+            pltpu.VMEM((4 * rows, 128), F32),
+            pltpu.VMEM((heads, 4 * rows, 3 * HEAD), BF16), pltpu.VMEM((heads, 4 * rows, 2 * HEAD), BF16),
+            pltpu.SemaphoreType.DMA((9,)),
+        ] + move_scratch(8),
+        compiler_params=pltpu.CompilerParams(
+            collective_id=4 * layer, has_side_effects=True, vmem_limit_bytes=VMEM_BYTES
+        ),
+        name="attend_fwd",
+    )(own, norm, w_qkv, w_out, f_qkv, f_out, w_in, w_down)
+    return result, (full, proj, ctx, lse, normed, scale), (f_in, f_down)
+
+
+def attend_bwd_kernel(
+    layer,
+    grad_ref, normed_ref, scale_ref, norm_ref, qkv_hbm, out_hbm, f_qkv, f_out, full_hbm, proj_hbm, ctx_hbm, lse_hbm,
+    sum_hbm, own_hbm, part_hbm,
+    grad_own, norm_grad, grads_hbm, got_hbm, owned_hbm,
+    full, part, core_in, chip_in, send, recv,
+    w_qkv, w_out, mid, proj, ctx, lse, gctx, dots, dproj, back_t, grads, sems,
+    move_send, move_recv, own_send, own_recv, own_load, acc,
+):
+    pair = Pair(full, part, core_in, chip_in, send, recv)
+    rows = pair.rows
+    inner = w_out.shape[0]
+    heads = inner // HEAD
+    loads = fetch((ctx_hbm, proj_hbm, lse_hbm, full_hbm), (ctx, proj, lse, mid), sems)
+    loads.append(load_quarter(out_hbm.at[layer], f_out, w_out, sems.at[4]))
+    loads.append(load_quarter(qkv_hbm.at[layer], f_qkv, w_qkv, sems.at[5]))
+    full[:rows] = ln_back(grad_ref[...], normed_ref, scale_ref, norm_ref, norm_grad)
+    job = PlaneSum(sum_hbm, got_hbm, FFN_ORDER, move_send, move_recv)
+    if layer == 0:
+        ship = OwnerSend(
+            own_hbm, part_hbm, acc, owned_hbm, ATT_ORDER, ATT_CHIP, ATT_UNIT, own_send, own_recv, own_load
+        )
+        ship.begin()
+    greet([pair.chip, *(sixteen() if layer == 0 else [pair.core, *near_chips()])], [])
+    pair.start()
+    if layer == 0:
+        ship.ship()
+    job.start()
+    for copy in loads:
+        copy.wait()
+    lanes = lax.broadcasted_iota(jnp.int32, (rows, 128), 1)
+    for tile in range(4):
+        span = tile_rows(tile, rows)
+        pair.arrive(tile)
+        grad_ctx = dot(full[span], w_out[...], NT)
+        gctx[span] = grad_ctx
+        products = grad_ctx * ctx[span]
+        sums = jnp.zeros((rows, 128), F32)
+        for head in range(heads):
+            cols = slice(head * HEAD, (head + 1) * HEAD)
+            sums = jnp.where(lanes == head, jnp.sum(products[:, cols], axis=1, keepdims=True), sums)
+        dots[span] = sums
+    block = 2 * rows
+    for head in range(heads):
+        cols = slice(head * HEAD, (head + 1) * HEAD)
+        key_high, key_low = halves(proj[1, :, cols])
+        keys = jnp.concatenate([key_high, key_low, key_high], axis=1)
+        keys_two = jnp.concatenate([key_high, key_low], axis=1)
+        high, low = halves(proj[2, :, cols])
+        values = jnp.concatenate([high, low, high], axis=1)
+        for step in range(2):
+            span = pl.ds(step * block, block)
+            query = proj[0, span, cols] * (HEAD ** -0.5)
+            high, low = halves(query)
+            scores = dot16(jnp.concatenate([high, high, low], axis=1), keys, NT)
+            probs = jnp.exp(scores - lse[span, head:head + 1])
+            upstream = gctx[span, cols]
+            high, low = halves(upstream)
+            grad_probs = dot16(jnp.concatenate([high, high, low], axis=1), values, NT)
+            grad_scores = probs * (grad_probs - dots[span, head:head + 1])
+            prob_high, prob_low = halves(probs)
+            up_high, up_low = halves(upstream.T)
+            mixed = dot16(jnp.concatenate([up_high, up_low], axis=0), prob_high, NN)
+            grad_v = mixed[:HEAD] + mixed[HEAD:] + dot16(up_high, prob_low, NN)
+            score_high, score_low = halves(grad_scores)
+            q_high, q_low = halves(query.T)
+            mixed = dot16(jnp.concatenate([q_high, q_low], axis=0), score_high, NN)
+            grad_k = mixed[:HEAD] + mixed[HEAD:] + dot16(q_high, score_low, NN)
+            mixed = dot16(score_high, keys_two, NN)
+            grad_q = mixed[:, :HEAD] + mixed[:, HEAD:] + dot16(score_low, key_high, NN)
+            dproj[0, span, cols] = grad_q * (HEAD ** -0.5)
+            if step == 0:
+                back_t[1, cols, :] = grad_k
+                back_t[2, cols, :] = grad_v
+            else:
+                back_t[1, cols, :] = back_t[1, cols, :] + grad_k
+                back_t[2, cols, :] = back_t[2, cols, :] + grad_v
+        dproj[1, :, cols] = back_t[1, cols, :].T
+        dproj[2, :, cols] = back_t[2, cols, :].T
+    for tile in (2, 3, 1, 0):
+        span = tile_rows(tile, rows)
+        part[span] = (
+            dot(dproj[0, span], w_qkv[0], NN) + dot(dproj[1, span], w_qkv[1], NN) + dot(dproj[2, span], w_qkv[2], NN)
+        )
+        pair.reduce(tile)
+    half = full.shape[1] // 2
+    grads[:inner] = dot(dproj[0], mid[...], TN)
+    middle = dot(back_t[1], mid[...], NN)
+    side = inner // 2
+    grads[inner:inner + side, :half] = middle[:side, :half]
+    grads[inner:inner + side, half:] = middle[side:, :half]
+    grads[inner + side:2 * inner, :half] = middle[:side, half:]
+    grads[inner + side:2 * inner, half:] = middle[side:, half:]
+    grads[2 * inner:3 * inner] = dot(back_t[2], mid[...], NN)
+    grads[3 * inner:] = dot(ctx[...], full[...], TN)
+    store = fetch((grads,), (grads_hbm,), sems, 6)[0]
+    pair.finish()
+    grad_own[...] = full[:rows] + pair.total()
+    store.wait()
+    job.finish()
+    if layer == 0:
+        ship.finish()
+
+
+def attend_bwd(grad, kept, w_qkv, w_out, f_qkv, f_out, to_sum, to_own, norm, layer):
+    full, proj, ctx, lse, normed, scale = kept
+    rows, width = grad.shape
+    inner = w_out.shape[1]
+    return pl.pallas_call(
+        functools.partial(attend_bwd_kernel, layer),
+        out_shape=(
+            shape(rows, width), shape(2, width), shape(4 * inner, width),
+            shape(3, to_sum.shape[0] // 4, width), shape(2, UNITS * BLOCK, width),
+        ),
+        in_specs=[VM] * 4 + [HB] * 11,
+        out_specs=(VM, VM, HB, HB, HB),
+        scratch_shapes=pair_scratch(rows, width) + [
+            pltpu.VMEM(w_qkv.shape[1:], F32), pltpu.VMEM(w_out.shape[1:], F32),
+            pltpu.VMEM((4 * rows, width), F32),
+            pltpu.VMEM(proj.shape, F32), pltpu.VMEM(ctx.shape, F32), pltpu.VMEM(lse.shape, F32),
+            pltpu.VMEM(ctx.shape, F32), pltpu.VMEM(lse.shape, F32), pltpu.VMEM(proj.shape, F32),
+            pltpu.VMEM((3, inner, 4 * rows), F32),
+            pltpu.VMEM((4 * inner, width), F32),
+            pltpu.SemaphoreType.DMA((7,)),
+        ] + own_scratch(inner, width),
+        compiler_params=pltpu.CompilerParams(
+            collective_id=4 * layer + 3, has_side_effects=True, vmem_limit_bytes=VMEM_BYTES
+        ),
+        name="attend_bwd",
+    )(grad, normed, scale, norm, w_qkv, w_out, f_qkv, f_out, full, proj, ctx, lse, to_sum, *to_own)
+
+
+def swap_partner(rows, home):
+    return jnp.where(home, rows, lax.ppermute(rows, ("c", "mh"), [(1, 2), (2, 1)]))
+
+
+def close_one_kernel(
+    sum_hbm, own_hbm, part_hbm, rows_hbm, norm_a, norm_b, norm_c, norm_d, params, moments,
+    got_hbm, owned_hbm, grad_hbm, norm_grads, moments_new, norms_new,
+    move_send, move_recv, own_send, own_recv, own_load, acc, swap_send, swap_recv, norm_in, norm_send, norm_recv,
+):
+    job = PlaneSum(sum_hbm, got_hbm, ATT_ORDER, move_send, move_recv)
+    ship = OwnerSend(own_hbm, part_hbm, acc, owned_hbm, FFN_ORDER, FFN_CHIP, FFN_UNIT, own_send, own_recv, own_load)
+    swap = Swap((rows_hbm,), (grad_hbm,), swap_send, swap_recv, 0)
+    ship.begin()
+    for i, ref in enumerate((norm_a, norm_b, norm_c, norm_d)):
+        norm_grads[2 * i:2 * i + 2] = ref[...]
+    e = lax.axis_index("e")
+    flips = [{axis: 1 - lax.axis_index(axis)} for axis in ("c", "ml", "mh")] + [{"e": beside(e, m)} for m in (1, 2)]
+    greet([flips[1], *sixteen()], [])
+    job.start()
+    swap.start()
+    for i, device in enumerate(flips):
+        copy = pltpu.make_async_remote_copy(
+            src_ref=norm_grads,
+            dst_ref=norm_in.at[i],
+            send_sem=norm_send.at[i],
+            recv_sem=norm_recv.at[i],
+            device_id=device,
+            device_id_type=MESH_ID,
+        )
+        copy.start()
+        if i == 0:
+            ship.ship()
+        copy.wait()
+        norm_grads[...] = norm_grads[...] + norm_in[i]
+    total = norm_grads[...]
+    moment = moment_decay * moments[...] + (1.0 - moment_decay) * total * total
+    moments_new[...] = moment
+    norms_new[...] = params[...] - vector_rate * total / (jnp.sqrt(moment) + vector_eps)
+    job.finish()
+    swap.finish()
+    ship.finish()
+
+
+def close_one(to_sum, to_own, rows, norms, params, moments):
+    width = rows.shape[1]
+    piece = to_own[0].shape[0] // 4
+    return pl.pallas_call(
+        close_one_kernel,
+        out_shape=(
+            shape(3, to_sum.shape[0] // 4, width), shape(2, UNITS * BLOCK, width), shape(*rows.shape),
+            shape(8, width), shape(8, width), shape(8, width),
+        ),
+        in_specs=[HB] * 4 + [VM] * 6,
+        out_specs=(HB, HB, HB, VM, VM, VM),
+        scratch_shapes=own_scratch(piece, width) + move_scratch(1)
+        + [pltpu.VMEM((5, 8, width), F32)] + move_scratch(5),
+        compiler_params=pltpu.CompilerParams(
+            collective_id=9, has_side_effects=True, vmem_limit_bytes=VMEM_BYTES
+        ),
+        name="close_one",
+    )(to_sum, *to_own, rows, *norms, params.reshape(8, width), moments.reshape(8, width))
+
+
+def close_two_kernel(
+    own_hbm, part_hbm, rows_hbm, owned_hbm, whole_hbm,
+    own_send, own_recv, own_load, acc, move_send, move_recv, sem,
+):
+    ship = OwnerSend(own_hbm, part_hbm, acc, owned_hbm, ATT_ORDER, ATT_CHIP, ATT_UNIT, own_send, own_recv, own_load)
+    job = PlaneGather(rows_hbm, whole_hbm, move_send, move_recv, sem)
+    ship.begin()
+    greet(sixteen(), [])
+    ship.ship()
+    job.start()
+    job.middle()
+    ship.finish()
+    job.finish()
+
+
+def close_two(to_own, rows):
+    width = rows.shape[1]
+    piece = to_own[0].shape[0] // 4
+    return pl.pallas_call(
+        close_two_kernel,
+        out_shape=(shape(2, UNITS * BLOCK, width), shape(8 * rows.shape[0], width)),
+        in_specs=[HB] * 3,
+        out_specs=(HB, HB),
+        scratch_shapes=own_scratch(piece, width)[2:] + move_scratch(10) + [pltpu.SemaphoreType.DMA],
+        compiler_params=pltpu.CompilerParams(
+            collective_id=10, has_side_effects=True, vmem_limit_bytes=VMEM_BYTES
+        ),
+        name="close_two",
+    )(*to_own, rows)
+
+
+def close_three_kernel(rows_hbm, whole_hbm, move_send, move_recv, sem):
+    job = PlaneGather(rows_hbm, whole_hbm, move_send, move_recv, sem)
+    greet([{"c": 1 - lax.axis_index("c")}, *near_chips()], [])
+    job.start()
+    job.middle()
+    job.finish()
+
+
+def close_three(rows):
+    return pl.pallas_call(
+        close_three_kernel,
+        out_shape=shape(8 * rows.shape[0], rows.shape[1]),
+        in_specs=[HB],
+        out_specs=HB,
+        scratch_shapes=move_scratch(10) + [pltpu.SemaphoreType.DMA],
+        compiler_params=pltpu.CompilerParams(collective_id=11, has_side_effects=True),
+        name="close_three",
+    )(rows)
+
+
+def shampoo_kernel(
+    layer,
+    ffn_ref, att_ref, qkv_hbm, out_hbm, in_hbm, down_hbm, left_ref, right_ref, left_root, right_root, *rest
+):
+    grads_ref, left_new, right_new, rows_ref, current, sems = rest[-6:]
+    owner = 2 * lax.axis_index("e") + lax.axis_index("c")
+    width = rows_ref.shape[1]
+    half = width // 2
+
+    def bring(source, row, col, cols, slot):
+        return pltpu.make_async_copy(
+            source, current.at[pl.ds(row, BLOCK), pl.ds(col, cols)], sems.at[slot]
+        )
+
+    def qkv_copies(who):
+        def part(c, i, col=None):
+            ref = qkv_hbm.at[layer, c, pl.ds(i * BLOCK, BLOCK)]
+            return ref if col is None else qkv_hbm.at[layer, c, pl.ds(i * BLOCK, BLOCK), pl.ds(col, half)]
+
+        mixed = 2 if who == 0 else 0
+        plain = [(0, 0), (0, 1)] if who == 0 else [(2, 0), (2, 1)]
+        copies = [bring(part(1, i, who * half), mixed * BLOCK, i * half, half, i) for i in range(2)]
+        for n, (c, i) in enumerate(plain):
+            row = (n if who == 0 else n + 1) * BLOCK
+            copies.append(bring(part(c, i), row, 0, width, 2 + n))
+        return copies
+
+    def wide_copy(source, first, s):
+        b = UNITS * owner + s - first
+        rows = pl.ds(pl.multiple_of(b * BLOCK, BLOCK), BLOCK)
+        return bring(source.at[layer, rows], s * BLOCK, 0, width, s)
+
+    for who in range(2):
+
+        @pl.when(owner == who)
+        def _():
+            copies = qkv_copies(who)
+            for copy in copies:
+                copy.start()
+            for copy in copies:
+                copy.wait()
+
+    @pl.when(owner >= 2)
+    def _():
+        for s in range(UNITS):
+            b = UNITS * owner + s
+            pl.when(b < 8)(lambda: wide_copy(out_hbm, 6, s).start())
+            pl.when(jnp.logical_and(b >= 8, b < 16))(lambda: wide_copy(in_hbm, 8, s).start())
+            pl.when(b >= 16)(lambda: wide_copy(down_hbm, 16, s).start())
+        for s in range(UNITS):
+            bring(current.at[pl.ds(0, BLOCK)], s * BLOCK, 0, width, s).wait()
+
+    def stripe(s, turned):
+        rows = pl.ds(pl.multiple_of(s * BLOCK, BLOCK), BLOCK)
+        ffn = UNITS * owner + s >= FFN_UNIT
+        summed = jnp.where(ffn, ffn_ref[0, rows] + ffn_ref[1, rows], att_ref[0, rows] + att_ref[1, rows])
+        old = current[rows]
+        fresh = []
+        for u in range(width // BLOCK):
+            cols = slice(u * BLOCK, (u + 1) * BLOCK)
+            tile = summed[:, cols]
+            if turned:
+                tile = tile.T
+                across = 2 * (u % 4) + u // 4
+                mixed = jnp.where(owner == 0, s == 2, s == 0)
+                n = jnp.where(
+                    mixed,
+                    jnp.where(owner == 0, 16, 0) + across,
+                    jnp.where(owner == 0, 0, 7) + 2 * u + s,
+                )
+            else:
+                n = s * (width // BLOCK) + u
+            grads_ref[n] = tile
+            left_new[n] = stat_decay * left_ref[n] + (1.0 - stat_decay) * dot(tile, tile, NT)
+            right_new[n] = stat_decay * right_ref[n] + (1.0 - stat_decay) * dot(tile, tile, TN)
+            step = dot(left_root[n], dot(tile, right_root[n], NN), NN)
+            size = jnp.mean(jnp.mean(step * step, axis=1, keepdims=True), axis=0, keepdims=True)
+            step = shampoo_rate * step * lax.rsqrt(size + graft_eps)
+            fresh.append(old[:, cols] - (step.T if turned else step))
+        rows_ref[rows] = jnp.concatenate(fresh, axis=1)
+
+    for turned in (True, False):
+
+        @pl.when(owner < 2 if turned else owner >= 2)
+        def _():
+            @pl.loop(0, UNITS)
+            def _(s):
+                stripe(s, turned)
+
+
+def shampoo(ffn_part, att_part, weights, stats, layer, earlier):
+    width = ffn_part.shape[2]
+    count = stats[0].shape[0] // 2
+    block = pl.BlockSpec((count, BLOCK, BLOCK), lambda i: (layer, 0, 0))
+    full = jax.ShapeDtypeStruct(stats[0].shape, F32)
+
+    def whole(*dims):
+        return pl.BlockSpec(dims, lambda i: (0,) * len(dims))
+
+    return pl.pallas_call(
+        functools.partial(shampoo_kernel, layer),
+        grid=(1,),
+        out_shape=(full, full, full, shape(UNITS * BLOCK, width)),
+        in_specs=[whole(*ffn_part.shape), whole(*att_part.shape)] + [HB] * 4 + [block] * 4 + [HB] * len(earlier),
+        out_specs=(block, block, block, whole(UNITS * BLOCK, width)),
+        scratch_shapes=[pltpu.VMEM((UNITS * BLOCK, width), F32), pltpu.SemaphoreType.DMA((4,))],
+        input_output_aliases={10 + i: i for i in range(len(earlier))},
+        compiler_params=pltpu.CompilerParams(vmem_limit_bytes=VMEM_BYTES),
+        name="shampoo",
+    )(ffn_part, att_part, *weights, *stats, *earlier)
+
+
+def unarrange(rows):
+    half = rows.shape[1] // 2
+    low, high = rows[192:288], rows[288:384]
+    mid = jnp.concatenate(
+        [
+            jnp.concatenate([low[:, :half], high[:, :half]], axis=1),
+            jnp.concatenate([low[:, half:], high[:, half:]], axis=1),
+        ],
+        axis=0,
+    )
+    return jnp.stack([rows[:192], mid, rows[384:576]]), rows[576:768], rows[768:1536], rows[1536:2304]
+
+
+def on_fine(
+    inputs,
+    cotangent,
+    loss_mask,
+    keep_mask,
+    w_qkv,
+    w_out,
+    w_in,
+    w_down,
+    norm_params,
+    norm_moments,
+    left_stats,
+    right_stats,
+    left_roots,
+    right_roots,
+):
+    home = lax.axis_index("c") == lax.axis_index("mh")
+    masked = cotangent * loss_mask.astype(jnp.float32)[:, None]
+    flag = jnp.broadcast_to(keep_mask.astype(jnp.float32)[:, None], (8, 128))
+    w_qkv = jnp.swapaxes(w_qkv, 2, 3)
+    hidden, f_qkv, f_out = open_step(inputs, w_qkv, w_out, 8)
+    used = []
+    kept = []
+    states = []
+    for layer in range(2):
+        middle, kept_a, (f_in, f_down) = attend_fwd(
+            hidden, w_qkv, w_out, f_qkv, f_out, w_in, w_down, norm_params[layer, 0], layer
+        )
+        used.append((f_qkv, f_out, f_in, f_down))
+        extra = (w_qkv, w_out) if layer == 0 else (masked, flag)
+        hidden, kept_f, got = ffn_fwd(
+            middle, w_in, w_down, f_in, f_down, extra, norm_params[layer, 1], layer, layer == 1
+        )
+        kept.append((kept_a, kept_f))
+        states.append(hidden)
+        f_qkv, f_out = got
+    masked, keep = got[0], got[1][0, 0]
+    outputs = swap_partner(states[0] + keep * (states[1] - states[0]), home)
+    grad = keep * masked
+    to_sum = to_own = None
+    owned, norms = [], []
+    for layer in (1, 0):
+        f_qkv, f_out, f_in, f_down = used[layer]
+        kept_a, kept_f = kept[layer]
+        grad_mid, norm_two, g_ffn, *moved = ffn_bwd(
+            grad, kept_f, w_in, w_down, f_in, f_down, to_sum, to_own, norm_params[layer, 1], layer
+        )
+        if layer == 0:
+            owned.append(moved[1])
+            to_own = (to_sum, moved[0])
+        else:
+            to_own = (g_ffn, g_ffn)
+        grad, norm_one, g_att, got, part = attend_bwd(
+            grad_mid, kept_a, w_qkv, w_out, f_qkv, f_out, g_ffn, to_own, norm_params[layer, 0], layer
+        )
+        if layer == 1:
+            grad = (1.0 - keep) * masked + grad
+        else:
+            owned.append(part)
+        norms = [norm_one, norm_two] + norms
+        to_sum, to_own = g_att, (g_ffn, got)
+    got, part, in_grads, norm_grads, moments_new, norms_new = close_one(
+        to_sum, to_own, grad, norms, norm_params, norm_moments
+    )
+    owned.append(part)
+    weights = (w_qkv, w_out, w_in, w_down)
+    stats = (left_stats, right_stats, left_roots, right_roots)
+    *blocks, renewed = shampoo(owned[0], owned[1], weights, stats, 1, ())
+    part, second = close_two((to_sum, got), renewed)
+    owned.append(part)
+    *blocks, renewed = shampoo(owned[2], owned[3], weights, stats, 0, blocks)
+    first = close_three(renewed)
+    fresh = [jnp.stack(pair) for pair in zip(unarrange(first), unarrange(second))]
+    fresh[0] = jnp.swapaxes(fresh[0], 2, 3)
+    like = norm_params.shape
+    return (
+        outputs, in_grads, *blocks, *fresh,
+        norm_grads.reshape(like), moments_new.reshape(like), norms_new.reshape(like),
+    )
+
+
+def fine_solution(mesh):
+    n_dp, n_mp = mesh.shape["dp"], mesh.shape["mp"]
+    fine = Mesh(mesh.devices.reshape(n_dp // 2, 2, n_mp // 2, 2), FINE)
+    rows, part = P(FINE, None), ("mh", "ml")
+    blocks = P(FINE, None, None)
+    weights = (P(None, None, None, part), P(None, part, None), P(None, None, part), P(None, part, None))
+    in_specs = (rows, rows, P(FINE), P(("e", "c")), *weights, P(), P(), blocks, blocks, blocks, blocks)
+    out_specs = (rows, rows, blocks, blocks, blocks, *weights, P(), P(), P())
+    return jax.shard_map(on_fine, mesh=fine, in_specs=in_specs, out_specs=out_specs, check_vma=False)
+
+
 def solution(mesh):
+    if mesh.shape["dp"] == 8 and mesh.shape["mp"] == 4:
+        return fine_solution(mesh)
+    return wide_solution(mesh)
+
+
+def wide_solution(mesh):
     in_specs = (
         P(("dp", "mp"), None),
         P(("dp", "mp"), None),

time: 1720 us -> 749 us (0.44)
  waiting for transfers between devices: 947 us -> 0.01 us
  Pallas kernels: 0 us -> 696 us
  matrix products: 380 us -> 0 us
  local copies, waits for them, and re-layouts: 246 us -> 17.9 us
  other arithmetic: 78.5 us -> 20.3 us
  blocking collectives: 45 us -> 0 us
    pallas_call x0 -> x14, Pallas kernels: none -> 696 us  [the longest x2 148 us: attend_bwd(): pl.pallas_call(functools.partial(attend_bwd_kernel, layer), out_shape=(sh...]
    all_gather x9 -> x0, waiting for transfers between devices: 529 us -> none  [the longest x4 254 us: gather_rows(): return lax.all_gather(local_rows, 'mp', axis=0, tiled=True)]
    reduce_scatter x8 -> x0, waiting for transfers between devices: 412 us -> none  [the longest x4 235 us: reduce_rows(): lax.psum_scatter(partial_value, 'mp', scatter_dimension=0, tiled=True)]
    dot_general x39 -> x0, matrix products: 372 us -> none  [the longest x6 56.3 us: matmul_t(): return jnp.einsum('sa,ba->sb', left_op, right_op, precision=HIGHEST)]
    reshape x22 -> x5, local copies, waits for them, and re-layouts: 79.2 us -> 3.13 us  [the longest x1 0.63 us: close_one(): moments.reshape(8, width)]
    another operation x26 -> x2, local copies, waits for them, and re-layouts: 60.9 us -> 6.91 us  [on_fine(): jnp.stack(pair)]
    unnamed x171 -> x19, local copies, waits for them, and re-layouts: 46.8 us -> 1.6 us
    psum x1 -> x0, blocking collectives: 45 us -> none  [on_device(): norm_grads = lax.psum(jnp.stack([norms_one, norms_two]), ('dp', 'mp'))]
  transfers between devices with their start and end apart: 18 -> 1, of which waited for: 16 -> 0; matrix products, arithmetic and copies ran while one was open for 14% -> 4% of each run, Pallas kernels for 0% -> 59%
where the time goes in v1:
time: 749 us; the launch traced here: 739 us
  Pallas kernels  696 us (93%)
  other arithmetic  20.3 us (3%)
  local copies, waits for them, and re-layouts  17.9 us (2%)
    pallas_call x2, Pallas kernels, attend_bwd(): pl.pallas_call(functools.partial(attend_bwd_kernel, layer), out_shape=(sh...  148 us
    pallas_call x2, Pallas kernels, attend_fwd(): pl.pallas_call(functools.partial(attend_fwd_kernel, layer), out_shape=(sh...  129 us
    pallas_call x2, Pallas kernels, ffn_bwd(): pl.pallas_call(functools.partial(ffn_bwd_kernel, layer), out_shape=(shape...  106 us
    pallas_call x2, Pallas kernels, ffn_fwd(): pl.pallas_call(functools.partial(ffn_fwd_kernel, layer, last), out_shape=...  105 us
    pallas_call x1, Pallas kernels, close_two(): pl.pallas_call(close_two_kernel, out_shape=(shape(2, UNITS * BLOCK, width...  62.5 us
    pallas_call x1, Pallas kernels, close_one(): pl.pallas_call(close_one_kernel, out_shape=(shape(3, to_sum.shape[0] // 4...  55.8 us
    pallas_call x1, Pallas kernels, close_three(): pl.pallas_call(close_three_kernel, out_shape=shape(8 * rows.shape[0], row...  36.9 us
    pallas_call x2, Pallas kernels, shampoo(): pl.pallas_call(functools.partial(shampoo_kernel, layer), grid=(1,), out_s...  28 us
  transfers between devices with their start and end apart: 1, of which 0 were waited for; matrix products, arithmetic and copies ran while one was open for 4% of the time, Pallas kernels for 59%

profile of v1, /device:TPU:0, one launch (start us, length us, event | category | flops | bytes accessed | tf_op | source)
XLA Modules:
  0.0 738.7 jit_solution(12852541481242343310)
XLA Ops:
  0.6 1.4 slice_bitcast_fusion.10
  3.3 2.1 broadcast_multiply_fusion.1.extra_a
  5.5 25.1 %open_step.1 = (f32[256,768]{1,0:T(8,128)}, f32[3,192,768]{2,1,0:T(8,128)}, f32[192,768]{1,0:T(8,128)}) custom-call(f32[256,768]{1,0:T(8,128)} %rows_hbm.1, f32[2,3,192,768]{3,2,1,0:T(8,128)} %bitcast.41, f32[2,192,768]{2,1,0:T(8,128)} %out_hbm.13), custom_call_target="tpu_custom_call" | custom-call | tf_op jit(solution)/shard_map/open_step/pallas_call | solution.py:792
  30.6 69.4 %attend_fwd.2 = (f32[256,768]{1,0:T(8,128)}, f32[256,768]{1,0:T(8,128)}, f32[256,128]{1,0:T(8,128)}, f32[1024,768]{1,0:T(8,128)}, f32[3,1024,192]{2,1,0:T(8,128)...) custom-call(f32[256,768]{1,0:T(8,128)} %get-tuple-element.82.own_ref, ...), custom_call_target="tpu_custom_call" | custom-call | tf_op jit(solution)/shard_map/attend_fwd/pallas_call | solution.py:1050
  99.9 55.2 %ffn_fwd.2 = (f32[256,768]{1,0:T(8,128)}, f32[256,768]{1,0:T(8,128)}, f32[256,128]{1,0:T(8,128)}, f32[1024,768]{1,0:T(8,128)}, f32[1024,768]{1,0:T(8,128)}, /*in...) custom-call(f32[256,768]{1,0:T(8,128)} %get-tuple-element.85.own_ref, ...), custom_call_target="tpu_custom_call" | custom-call | tf_op jit(solution)/shard_map/ffn_fwd/pallas_call | solution.py:860
  155.1 59.8 %attend_fwd.3 = (f32[256,768]{1,0:T(8,128)}, f32[256,768]{1,0:T(8,128)}, f32[256,128]{1,0:T(8,128)}, f32[1024,768]{1,0:T(8,128)}, f32[3,1024,192]{2,1,0:T(8,128)...) custom-call(f32[256,768]{1,0:T(8,128)} %get-tuple-element.88.own_ref, ...), custom_call_target="tpu_custom_call" | custom-call | tf_op jit(solution)/shard_map/attend_fwd/pallas_call | solution.py:1050
  215.5 49.9 %ffn_fwd.3 = (f32[256,768]{1,0:T(8,128)}, f32[256,768]{1,0:T(8,128)}, f32[256,128]{1,0:T(8,128)}, f32[1024,768]{1,0:T(8,128)}, f32[1024,768]{1,0:T(8,128)}, /*in...) custom-call(f32[256,768]{1,0:T(8,128)} %get-tuple-element.91.own_ref, ...), custom_call_target="tpu_custom_call" | custom-call | tf_op jit(solution)/shard_map/ffn_fwd/pallas_call | solution.py:860
  265.4 1.3 slice.89
  266.7 1.9 multiply_add_fusion.1
  268.6 1.6 collective-permute-start
  270.8 1.6 broadcast_multiply_fusion.grad_ref
  273.6 52.3 %ffn_bwd.2 = (f32[256,768]{1,0:T(8,128)}, f32[2,768]{1,0:T(2,128)}, f32[1536,768]{1,0:T(8,128)}) custom-call(f32[256,768]{1,0:T(8,128)} %broadcast_multiply_fusion.grad_ref, f32[256,768]{1,0:T(8,128)} %get-tuple-element.97.normed_ref, f32[256,128]{1,0:T(8,128)} %get-tuple-element.98.scale_ref, f32[2,768]{1,0:T(2,128)} %get-tuple-element.170.norm_ref, ...), custom_call_target="tpu_custom_call" | custom-call | tf_op jit(solution)/shard_map/ffn_bwd/pallas_call | solution.py:960
  325.9 59.9 %attend_bwd.2 = (f32[256,768]{1,0:T(8,128)}, f32[2,768]{1,0:T(2,128)}, f32[768,768]{1,0:T(8,128)}, f32[3,384,768]{2,1,0:T(8,128)}, f32[2,288,768]{2,1,0:T(8,128)}) custom-call(f32[256,768]{1,0:T(8,128)} %get-tuple-element.102.grad_ref, f32[256,768]{1,0:T(8,128)} %get-tuple-element.103.normed_ref, f32[256,128]{1,0:T(8,128)} %get-tuple-element.104.scale_ref, ...), custom_call_target="tpu_custom_call" | custom-call | tf_op jit(solution)/shard_map/attend_bwd/pallas_call | solution.py:1182
  385.8 2.1 multiply_add_fusion.grad_ref
  387.9 53.7 %ffn_bwd.3 = (f32[256,768]{1,0:T(8,128)}, f32[2,768]{1,0:T(2,128)}, f32[1536,768]{1,0:T(8,128)}, f32[3,192,768]{2,1,0:T(8,128)}, f32[2,288,768]{2,1,0:T(8,128)}) custom-call(f32[256,768]{1,0:T(8,128)} %multiply_add_fusion.grad_ref, f32[256,768]{1,0:T(8,128)} %get-tuple-element.111.normed_ref, f32[256,128]{1,0:T(8,128)} %get-tuple-element.112.scale_ref, ...), custom_call_target="tpu_custom_call" | custom-call | tf_op jit(solution)/shard_map/ffn_bwd/pallas_call | solution.py:960
  441.6 87.8 %attend_bwd.3 = (f32[256,768]{1,0:T(8,128)}, f32[2,768]{1,0:T(2,128)}, f32[768,768]{1,0:T(8,128)}, f32[3,384,768]{2,1,0:T(8,128)}, f32[2,288,768]{2,1,0:T(8,128)}) custom-call(f32[256,768]{1,0:T(8,128)} %get-tuple-element.118.grad_ref, f32[256,768]{1,0:T(8,128)} %get-tuple-element.119.normed_ref, f32[256,128]{1,0:T(8,128)} %get-tuple-element.120.scale_ref, ...), custom_call_target="tpu_custom_call" | custom-call | tf_op jit(solution)/shard_map/attend_bwd/pallas_call | solution.py:1182
  529.5 14.1 %shampoo.2 = (f32[48,96,96]{2,1,0:T(8,128)}, f32[48,96,96]{2,1,0:T(8,128)}, f32[48,96,96]{2,1,0:T(8,128)}, f32[288,768]{1,0:T(8,128)}) custom-call(f32[2,288,768]{2,1,0:T(8,128)} %get-tuple-element.137.ffn_ref, f32[2,288,768]{2,1,0:T(8,128)} %get-tuple-element.138.att_ref, f32[2,3,192,768]{3,2,1,0:T(8,128)} %bitcast.47, f32[2,192,768]{2,1,0:T(8,128)} %out_hbm.13, ...), custom_call_target="tpu_custom_call" | custom-call | tf_op jit(solution)/shard_map/shampoo/pallas_call | solution.py:1419
  543.6 55.8 %close_one.1 = (f32[3,192,768]{2,1,0:T(8,128)}, f32[2,288,768]{2,1,0:T(8,128)}, f32[256,768]{1,0:T(8,128)}, f32[8,768]{1,0:T(8,128)}, f32[8,768]{1,0:T(8,128)}, /*index=5*/f32[8,768]{1,0:T(8,128)}) custom-call(f32[768,768]{1,0:T(8,128)} %get-tuple-element.127.sum_hbm.own_hbm, f32[1536,768]{1,0:T(8,128)} %get-tuple-element.125.sum_hbm.own_hbm, ...), custom_call_target="tpu_custom_call" | custom-call | tf_op jit(solution)/shard_map/close_one/pallas_call | solution.py:1252
  599.5 62.5 %close_two.1 = (f32[2,288,768]{2,1,0:T(8,128)}, f32[2304,768]{1,0:T(8,128)}) custom-call(f32[768,768]{1,0:T(8,128)} %get-tuple-element.127.sum_hbm.own_hbm, f32[3,192,768]{2,1,0:T(8,128)} %get-tuple-element.136.part_hbm, f32[288,768]{1,0:T(8,128)} %get-tuple-element.139.rows_hbm), custom_call_target="tpu_custom_call" | custom-call | tf_op jit(solution)/shard_map/close_two/pallas_call | solution.py:1287
  662.0 1.9 fusion.1
  663.9 4.1 slice_bitcast_fusion
  668.0 13.9 %shampoo.3 = (f32[48,96,96]{2,1,0:T(8,128)}, f32[48,96,96]{2,1,0:T(8,128)}, f32[48,96,96]{2,1,0:T(8,128)}, f32[288,768]{1,0:T(8,128)}) custom-call(f32[2,288,768]{2,1,0:T(8,128)} %get-tuple-element.135.ffn_ref, f32[2,288,768]{2,1,0:T(8,128)} %get-tuple-element.140.att_ref, ...), custom_call_target="tpu_custom_call", output_to_operand_aliasing={{0}: (10, {}), {1}: (11, {}), {2}: (12, {})} | custom-call | tf_op jit(solution)/shard_map/shampoo/pallas_call | solution.py:1419
  681.9 36.9 %close_three.1 = f32[2304,768]{1,0:T(8,128)} custom-call(f32[288,768]{1,0:T(8,128)} %get-tuple-element.147.rows_hbm), custom_call_target="tpu_custom_call" | custom-call | tf_op jit(solution)/shard_map/close_three/pallas_call | solution.py:1309
  718.8 1.2 fusion
  720.0 1.7 slice_bitcast_fusion.4
  721.8 1.6 slice_bitcast_fusion.5
  723.6 2.0 maximum_bitcast_fusion
  725.6 1.1 pad_maximum_fusion.2
  728.6 2.8 slice_bitcast_fusion.1
  731.7 4.3 pad_maximum_fusion
  736.0 1.0 broadcast_select_fusion
  737.4 0.9 copy.34
  (28 shorter events, 5.4 us)
Async XLA Ops:
  215.5 51.2 %copy-start.1 = (f32[256,768]{1,0:T(8,128)S(1)}, f32[256,768]{1,0:T(8,128)}, u32[]{:S(2)}) copy-start(f32[256,768]{1,0:T(8,128)} %get-tuple-element.88.own_ref) | copy-start | bytes 2359300
  265.4 4.7 copy-start.4
  265.4 5.3 copy-start.2
  265.4 7.6 %copy-start.5 = (f32[2,2,2,768]{3,2,1,0:T(2,128)S(1)}, f32[2,2,2,768]{3,2,1,0:T(2,128)}, u32[]{:S(2)}) copy-start(f32[2,2,2,768]{3,2,1,0:T(2,128)} %param.23) | copy-start | bytes 73732
  268.6 467.4 %collective-permute-start = (f32[256,768]{1,0:T(8,128)S(1)}, f32[256,768]{1,0:T(8,128)}, u32[]{:S(2)}, u32[]{:S(2)}) collective-permute-start(f32[256,768]{1,0:T(8,128)S(1)} %multiply_add_fusion.1), channel_id=1, source_target_pairs={{2,4},{4,2},{3,5},{5,3},{10,12},{12,10},{11,13},{13,11},{18,20},{2... | collective-permute-start | bytes 2359304 | tf_op jit(solution)/shard_map/ppermute | solution.py:1207
  725.6 1.1 copy-start.8
  725.6 1.7 copy-start.7
  725.6 2.4 copy-start.6
  728.6 3.1 copy-start
  736.0 1.4 copy-start.3
